TPU v7x, 512 devices: a whole 4x8x8 slice. The times are simulated.
512 devices in a mesh: section: 8 (over x, core), dp: 32 (over y_hi, z), tensor: 2 (over y_lo).
Axes of the slice: x: 4, y: 8 (y_hi: 4, y_lo: 2; y = y_hi * 2 + y_lo), z: 8, core: 2. Of those that a mesh axis runs over, the one named last changes fastest.
Arguments:
- embeddings: bfloat16 [4096, 1024], P('dp'), may hold values from -6 to 6
- cotangent: bfloat16 [4096, 1024], P('dp'), may hold values from -6 to 6
- w_up: bfloat16 [8, 1024, 2048], P('section', 'dp', 'tensor'), may hold values from -0.1875 to 0.1875
- w_down: bfloat16 [8, 2048, 1024], P('section', 'tensor', 'dp'), may hold values from -0.125 to 0.125
- b_up: float32 [8, 2048], P('section', 'tensor'), may hold values from -3 to 3
- b_down: float32 [8, 1024], P('section'), may hold values from -3 to 3
- ln_gain: float32 [8, 1024], P('section'), may hold values from 0.5 to 1.5
- ln_bias: float32 [8, 1024], P('section'), may hold values from -2 to 2
- fwd_store: bfloat16 [8, 64, 128, 1024], P('section', 'dp'), may hold values from -6 to 6
- bwd_store: bfloat16 [8, 64, 128, 1024], P('section', 'dp'), may hold values from -6 to 6
- sample_ids: int32 [32], P('dp'), may hold values from 0 to 1
- fwd_scales: int32 [8, 4096, 8], P('section', 'dp'), may hold values from 1 to 8
- bwd_scales: int32 [8, 4096, 8], P('section', 'dp'), may hold values from 1 to 8
Outputs:
- layer_outs: bfloat16 [8, 4096, 1024], P('section', 'dp')
- input_grads: bfloat16 [8, 4096, 1024], P('section', 'dp')
- grad_up: float32 [8, 1024, 2048], P('section', 'dp', 'tensor')
- grad_down_t: float32 [8, 1024, 2048], P('section', 'dp', 'tensor')
All inputs are finite; a program needn't handle non-finite values.
Results may differ from a plain program's by a relative error of at most 0.035.
Values may be sent and summed in bfloat16 or wider, within the bound.
A program may use at most 64 MiB of HBM per device.

v0:
```python
import jax
import jax.numpy as jnp
from jax import lax
from jax.sharding import PartitionSpec as P

root_half = 0.7071067811865476
density = 0.3989422804014327
epsilon = 1e-05


def passed_along(block, axis, distance):
    devices = range(lax.axis_size(axis))
    route = [(i - distance, i) for i in devices if i - distance in devices]
    return lax.ppermute(block, axis, route)


def gelu_value(pre_gelu):
    return pre_gelu * 0.5 * (1.0 + lax.erf(pre_gelu * root_half))


def gelu_slope(pre_gelu):
    return (
        0.5 * (1.0 + lax.erf(pre_gelu * root_half))
        + pre_gelu * jnp.exp(-0.5 * pre_gelu * pre_gelu) * density
    )


def normalize(inputs):
    values = inputs.astype(jnp.float32)
    centered = values - jnp.mean(values, axis=-1, keepdims=True)
    inverse = lax.rsqrt(jnp.mean(centered * centered, axis=-1, keepdims=True) + epsilon)
    return (centered * inverse, inverse)


def norm_backward(inputs, norm_gain, upstream):
    unit_values, inverse = normalize(inputs)
    scaled = upstream * norm_gain
    first_mean = jnp.mean(scaled, axis=-1, keepdims=True)
    second_mean = jnp.mean(scaled * unit_values, axis=-1, keepdims=True)
    return inverse * (scaled - first_mean - unit_values * second_mean)


def coded(values, stored_rows, scale_rows):
    block_count = scale_rows.shape[-1]
    bound_rows = 0.25 * jnp.repeat(
        scale_rows.astype(jnp.float32), values.shape[-1] // block_count, axis=-1
    )
    base_values = stored_rows.astype(jnp.float32)
    return (
        base_values + jnp.clip(values.astype(jnp.float32) - base_values, -bound_rows, bound_rows)
    ).astype(jnp.bfloat16)


def inner(left, right):
    return lax.dot_general(
        left, right, (((0,), (0,)), ((), ())), preferred_element_type=jnp.float32
    )


def outer_t(left, right):
    return lax.dot_general(
        left, right, (((1,), (1,)), ((), ())), preferred_element_type=jnp.float32
    )


def share_terms(accums):
    up_rows = accums[0]
    down_rows = accums[1]
    narrow = lax.optimization_barrier(jnp.stack([up_rows, down_rows], 1).astype(jnp.bfloat16))
    return narrow.astype(jnp.float32)


def per_device(
    embeddings,
    cotangent,
    w_up,
    w_down,
    b_up,
    b_down,
    ln_gain,
    ln_bias,
    fwd_store,
    bwd_store,
    sample_ids,
    fwd_scales,
    bwd_scales,
):
    section_count = lax.axis_size("section")
    section_index = lax.axis_index("section")
    token_rows, width = embeddings.shape
    seq_rows = fwd_store.shape[2]
    micro_count = sample_ids.shape[0]
    hidden_units = w_up.shape[2]
    step_count = micro_count + section_count - 1
    up_whole, down_whole = (
        lax.all_gather(w_up, "dp", axis=1, tiled=True),
        lax.all_gather(w_down, "dp", axis=2, tiled=True),
    )
    up_full = up_whole[0]
    down_full = down_whole[0]
    norm_gain = ln_gain[0]
    norm_bias = ln_bias[0]
    up_bias = b_up[0]
    down_bias = b_down[0]
    out_store = fwd_store[0]
    back_store = bwd_store[0]
    out_scales = fwd_scales[0]
    back_scales = bwd_scales[0]

    def place(buffer, fresh, active):
        return jnp.where(active, fresh, buffer)

    def forward_run(inputs):
        unit_values, _ = normalize(inputs)
        normed = (unit_values * norm_gain + norm_bias).astype(jnp.bfloat16)
        pre_gelu = jnp.dot(normed, up_full, preferred_element_type=jnp.float32) + up_bias
        activated = gelu_value(pre_gelu).astype(jnp.bfloat16)
        partial_value = jnp.dot(activated, down_full, preferred_element_type=jnp.float32)
        return (normed, pre_gelu, activated, partial_value)

    def forward_skip(inputs):
        return (
            jnp.zeros((seq_rows, width), jnp.bfloat16),
            jnp.zeros((seq_rows, hidden_units), jnp.float32),
            jnp.zeros((seq_rows, hidden_units), jnp.bfloat16),
            jnp.zeros((seq_rows, width), jnp.float32),
        )

    def forward_step(step_index, carry):
        incoming, outputs, kept_inputs, kept_normed, kept_pre, kept_act = carry
        micro_index = step_index - section_index
        active = (micro_index >= 0) & (micro_index < micro_count)
        micro_slot = jnp.clip(micro_index, 0, micro_count - 1)
        row_start = micro_slot * seq_rows
        inputs = jnp.where(section_index == 0, embeddings, incoming)
        normed, pre_gelu, activated, partial_value = lax.cond(
            active, forward_run, forward_skip, inputs
        )
        summed = lax.psum(partial_value.astype(jnp.bfloat16), "tensor").astype(jnp.float32)
        output = (inputs.astype(jnp.float32) + summed + down_bias).astype(jnp.bfloat16)
        stored_rows = lax.dynamic_index_in_dim(out_store, sample_ids[micro_slot], 0, keepdims=False)
        coded_rows = coded(output, stored_rows, out_scales)
        outputs = place(outputs, output, active)
        kept_inputs = place(kept_inputs, inputs, active)
        kept_normed = place(kept_normed, normed, active)
        kept_pre = place(kept_pre, pre_gelu, active)
        kept_act = place(kept_act, activated, active)
        incoming = passed_along(coded_rows, "section", 1)
        return (incoming, outputs, kept_inputs, kept_normed, kept_pre, kept_act)

    empty_act = jnp.zeros((token_rows, width), jnp.bfloat16)
    forward_start = (
        jnp.zeros((seq_rows, width), jnp.bfloat16),
        empty_act,
        empty_act,
        empty_act,
        jnp.zeros((token_rows, hidden_units), jnp.float32),
        jnp.zeros((token_rows, hidden_units), jnp.bfloat16),
    )
    forward_end = lax.fori_loop(0, step_count, forward_step, forward_start)
    _, outputs, kept_inputs, kept_normed, kept_pre, kept_act = forward_end

    def backward_run(operand):
        upstream, row_start, accum_up, accum_down = operand
        down_term = inner(upstream, kept_act)
        act_grad = outer_t(upstream, down_full)
        pre_grad = (act_grad * gelu_slope(kept_pre)).astype(jnp.bfloat16)
        up_term = inner(kept_normed, pre_grad)
        partial_value = outer_t(pre_grad, up_full)
        return (partial_value, accum_up + up_term, accum_down + down_term)

    def backward_skip(operand):
        upstream, row_start, accum_up, accum_down = operand
        return (jnp.zeros((seq_rows, width), jnp.float32), accum_up, accum_down)

    def backward_step(step_index, carry):
        incoming, input_grads, accum_up, accum_down = carry
        micro_index = step_index - (section_count - 1 - section_index)
        active = (micro_index >= 0) & (micro_index < micro_count)
        micro_slot = jnp.clip(micro_index, 0, micro_count - 1)
        row_start = micro_slot * seq_rows
        upstream = jnp.where(section_index == section_count - 1, cotangent, incoming)
        partial_value, accum_up, accum_down = lax.cond(
            active, backward_run, backward_skip, (upstream, row_start, accum_up, accum_down)
        )
        norm_grad = lax.psum(partial_value.astype(jnp.bfloat16), "tensor").astype(jnp.float32)
        input_grad = (
            upstream.astype(jnp.float32) + norm_backward(kept_inputs, norm_gain, norm_grad)
        ).astype(jnp.bfloat16)
        stored_rows = lax.dynamic_index_in_dim(
            back_store, sample_ids[micro_slot], 0, keepdims=False
        )
        coded_rows = coded(input_grad, stored_rows, back_scales)
        input_grads = place(input_grads, input_grad, active)
        incoming = passed_along(coded_rows, "section", -1)
        return (incoming, input_grads, accum_up, accum_down)

    backward_start = (
        jnp.zeros((seq_rows, width), jnp.bfloat16),
        empty_act,
        jnp.zeros((width, hidden_units), jnp.float32),
        jnp.zeros((width, hidden_units), jnp.float32),
    )
    backward_end = lax.fori_loop(0, step_count, backward_step, backward_start)
    _, input_grads, accum_up, accum_down = backward_end
    reduced = lax.psum_scatter(
        share_terms((accum_up, accum_down)).astype(jnp.bfloat16),
        "dp",
        scatter_dimension=0,
        tiled=True,
    ).astype(jnp.float32)
    return (outputs[None], input_grads[None], reduced[:, 0][None], reduced[:, 1][None])


def solution(mesh):
    return jax.shard_map(
        per_device,
        mesh=mesh,
        in_specs=(
            P("dp", None),
            P("dp", None),
            P("section", "dp", "tensor"),
            P("section", "tensor", "dp"),
            P("section", "tensor"),
            P("section", None),
            P("section", None),
            P("section", None),
            P("section", "dp", None, None),
            P("section", "dp", None, None),
            P("dp"),
            P("section", "dp", None),
            P("section", "dp", None),
        ),
        out_specs=(
            P("section", "dp", None),
            P("section", "dp", None),
            P("section", "dp", "tensor"),
            P("section", "dp", "tensor"),
        ),
        check_vma=False,
    )
```

profile of v0, /device:TPU:6, one launch (start us, length us, event | category | flops | bytes accessed | tf_op | source)
XLA Modules:
  0.0 1372.1 jit_solution(12046166019805161687)
XLA Ops:
  12.9 89.1 %all-gather.5.cloned.1.call-done = bf16[1,1024,1024]{1,2,0:T(8,128)(2,1)} async-done(((bf16[1,1024,32]{1,2,0:T(8,128)(2,1)}), bf16[1,1024,1024]{1,2,0:T(8,128)(2,1)}) %all-gather.5.cloned.1.call-update) | async-done | bytes 2097168 | tf_op jit(solution)/shard_map/all_gather | solution.py:97
  102.0 2.9 copy.23
  104.8 82.6 %all-gather.3.cloned.1.call-done = bf16[1,1024,1024]{2,1,0:T(8,128)(2,1)} async-done(((bf16[1,32,1024]{2,1,0:T(8,128)(2,1)}), bf16[1,1024,1024]{2,1,0:T(8,128)(2,1)}) %all-gather.3.cloned.1.call-update) | async-done | bytes 2097168 | tf_op jit(solution)/shard_map/all_gather | solution.py:96
  187.5 433.7 %while.48 = (s32[]{:T(128)}, bf16[128,1024]{1,0:T(8,128)(2,1)S(1)}, bf16[128,1024]{1,0:T(8,128)(2,1)}, bf16[128,1024]{1,0:T(8,128)(2,1)S(1)}, bf16[128,1024]{1,0...) while((s32[]{:T(128)}, bf16[128,1024]{1,0:T(8,128)(2,1)S(1)}, ...), condition=%wide.region_6.7_spmd.clone, body=%wide.region_0.6_spmd.clone.sunk | while | flops 543294592 | bytes 18125708 | solution.py:160
  187.7 2.4 conditional.6
  191.8 37.2 %all-reduce.3.cloned.1.call-done = bf16[128,1024]{1,0:T(8,128)(2,1)} async-done(((bf16[128,1024]{1,0:T(8,128)(2,1)}), bf16[128,1024]{1,0:T(8,128)(2,1)}) %all-reduce.3.cloned.1.call-update) | async-done | bytes 262160 | tf_op jit(solution)/shard_map/while/body/eval_jaxpr/psum | solution.py:139
  235.0 3.1 collective-permute-done
  238.3 2.4 conditional.6
  243.4 38.8 %all-reduce.3.cloned.1.call-done = bf16[128,1024]{1,0:T(8,128)(2,1)} async-done(((bf16[128,1024]{1,0:T(8,128)(2,1)}), bf16[128,1024]{1,0:T(8,128)(2,1)}) %all-reduce.3.cloned.1.call-update) | async-done | bytes 262160 | tf_op jit(solution)/shard_map/while/body/eval_jaxpr/psum | solution.py:139
  289.3 2.1 collective-permute-done
  291.5 2.4 conditional.6
  296.6 40.4 %all-reduce.3.cloned.1.call-done = bf16[128,1024]{1,0:T(8,128)(2,1)} async-done(((bf16[128,1024]{1,0:T(8,128)(2,1)}), bf16[128,1024]{1,0:T(8,128)(2,1)}) %all-reduce.3.cloned.1.call-update) | async-done | bytes 262160 | tf_op jit(solution)/shard_map/while/body/eval_jaxpr/psum | solution.py:139
  344.1 2.1 collective-permute-done
  346.4 2.4 conditional.6
  351.5 39.6 %all-reduce.3.cloned.1.call-done = bf16[128,1024]{1,0:T(8,128)(2,1)} async-done(((bf16[128,1024]{1,0:T(8,128)(2,1)}), bf16[128,1024]{1,0:T(8,128)(2,1)}) %all-reduce.3.cloned.1.call-update) | async-done | bytes 262160 | tf_op jit(solution)/shard_map/while/body/eval_jaxpr/psum | solution.py:139
  398.2 2.1 collective-permute-done
  400.4 2.4 conditional.6
  405.5 42.0 %all-reduce.3.cloned.1.call-done = bf16[128,1024]{1,0:T(8,128)(2,1)} async-done(((bf16[128,1024]{1,0:T(8,128)(2,1)}), bf16[128,1024]{1,0:T(8,128)(2,1)}) %all-reduce.3.cloned.1.call-update) | async-done | bytes 262160 | tf_op jit(solution)/shard_map/while/body/eval_jaxpr/psum | solution.py:139
  454.6 2.1 collective-permute-done
  456.8 2.4 conditional.6
  461.9 40.8 %all-reduce.3.cloned.1.call-done = bf16[128,1024]{1,0:T(8,128)(2,1)} async-done(((bf16[128,1024]{1,0:T(8,128)(2,1)}), bf16[128,1024]{1,0:T(8,128)(2,1)}) %all-reduce.3.cloned.1.call-update) | async-done | bytes 262160 | tf_op jit(solution)/shard_map/while/body/eval_jaxpr/psum | solution.py:139
  509.8 2.1 collective-permute-done
  512.0 5.8 conditional.6
  513.3 3.1 multiply_convert_fusion
  518.6 2.1 select_select_fusion.14
  520.7 38.1 %all-reduce.3.cloned.1.call-done = bf16[128,1024]{1,0:T(8,128)(2,1)} async-done(((bf16[128,1024]{1,0:T(8,128)(2,1)}), bf16[128,1024]{1,0:T(8,128)(2,1)}) %all-reduce.3.cloned.1.call-update) | async-done | bytes 262160 | tf_op jit(solution)/shard_map/while/body/eval_jaxpr/psum | solution.py:139
  562.2 2.0 select_select_fusion.13
  568.1 2.4 conditional.6
  573.2 38.8 %all-reduce.3.cloned.1.call-done = bf16[128,1024]{1,0:T(8,128)(2,1)} async-done(((bf16[128,1024]{1,0:T(8,128)(2,1)}), bf16[128,1024]{1,0:T(8,128)(2,1)}) %all-reduce.3.cloned.1.call-update) | async-done | bytes 262160 | tf_op jit(solution)/shard_map/while/body/eval_jaxpr/psum | solution.py:139
  619.1 2.1 collective-permute-done
  622.5 2.5 broadcast.152
  625.0 2.5 broadcast.152.clone
  627.5 494.3 %while.49 = (s32[]{:T(128)}, bf16[128,1024]{1,0:T(8,128)(2,1)S(1)}, bf16[128,1024]{1,0:T(8,128)(2,1)}, f32[1024,1024]{0,1:T(8,128)}, f32[1024,1024]{1,0:T(8,128)...) while((s32[]{:T(128)}, bf16[128,1024]{1,0:T(8,128)(2,1)S(1)}, ...), condition=%wide.region_15.16_spmd.clone, body=%wide.region_7.15_spmd.clone.sunk | while | flops 1082131584 | bytes 66090984 | solution.py:204
  628.8 48.5 %all-reduce.5.cloned.1.call-done = bf16[128,1024]{1,0:T(8,128)(2,1)} async-done(((bf16[128,1024]{1,0:T(8,128)(2,1)}), bf16[128,1024]{1,0:T(8,128)(2,1)}) %all-reduce.5.cloned.1.call-update) | async-done | bytes 262160 | tf_op jit(solution)/shard_map/while/body/eval_jaxpr/psum | solution.py:186
  678.5 2.0 select_select_fusion.15
  683.8 3.9 collective-permute-done.1
  687.7 11.3 conditional.7
  687.7 2.5 fusion.6
  690.2 5.0 bitcast_add_fusion
  700.1 39.9 %all-reduce.5.cloned.1.call-done = bf16[128,1024]{1,0:T(8,128)(2,1)} async-done(((bf16[128,1024]{1,0:T(8,128)(2,1)}), bf16[128,1024]{1,0:T(8,128)(2,1)}) %all-reduce.5.cloned.1.call-update) | async-done | bytes 262160 | tf_op jit(solution)/shard_map/while/body/eval_jaxpr/psum | solution.py:186
  741.1 2.1 select_select_fusion.15
  746.5 3.9 collective-permute-done.1
  751.5 52.4 %all-reduce.5.cloned.1.call-done = bf16[128,1024]{1,0:T(8,128)(2,1)} async-done(((bf16[128,1024]{1,0:T(8,128)(2,1)}), bf16[128,1024]{1,0:T(8,128)(2,1)}) %all-reduce.5.cloned.1.call-update) | async-done | bytes 262160 | tf_op jit(solution)/shard_map/while/body/eval_jaxpr/psum | solution.py:186
  805.2 2.1 select_select_fusion.15
  810.5 3.9 collective-permute-done.1
  815.6 51.4 %all-reduce.5.cloned.1.call-done = bf16[128,1024]{1,0:T(8,128)(2,1)} async-done(((bf16[128,1024]{1,0:T(8,128)(2,1)}), bf16[128,1024]{1,0:T(8,128)(2,1)}) %all-reduce.5.cloned.1.call-update) | async-done | bytes 262160 | tf_op jit(solution)/shard_map/while/body/eval_jaxpr/psum | solution.py:186
  868.2 2.1 select_select_fusion.15
  873.5 3.9 collective-permute-done.1
  878.6 51.2 %all-reduce.5.cloned.1.call-done = bf16[128,1024]{1,0:T(8,128)(2,1)} async-done(((bf16[128,1024]{1,0:T(8,128)(2,1)}), bf16[128,1024]{1,0:T(8,128)(2,1)}) %all-reduce.5.cloned.1.call-update) | async-done | bytes 262160 | tf_op jit(solution)/shard_map/while/body/eval_jaxpr/psum | solution.py:186
  931.0 2.1 select_select_fusion.15
  936.4 3.9 collective-permute-done.1
  941.5 49.8 %all-reduce.5.cloned.1.call-done = bf16[128,1024]{1,0:T(8,128)(2,1)} async-done(((bf16[128,1024]{1,0:T(8,128)(2,1)}), bf16[128,1024]{1,0:T(8,128)(2,1)}) %all-reduce.5.cloned.1.call-update) | async-done | bytes 262160 | tf_op jit(solution)/shard_map/while/body/eval_jaxpr/psum | solution.py:186
  992.5 2.1 select_select_fusion.15
  997.9 3.9 collective-permute-done.1
  1002.9 50.3 %all-reduce.5.cloned.1.call-done = bf16[128,1024]{1,0:T(8,128)(2,1)} async-done(((bf16[128,1024]{1,0:T(8,128)(2,1)}), bf16[128,1024]{1,0:T(8,128)(2,1)}) %all-reduce.5.cloned.1.call-update) | async-done | bytes 262160 | tf_op jit(solution)/shard_map/while/body/eval_jaxpr/psum | solution.py:186
  1054.5 2.1 select_select_fusion.15
  1059.8 3.9 collective-permute-done.1
  1064.9 46.6 %all-reduce.5.cloned.1.call-done = bf16[128,1024]{1,0:T(8,128)(2,1)} async-done(((bf16[128,1024]{1,0:T(8,128)(2,1)}), bf16[128,1024]{1,0:T(8,128)(2,1)}) %all-reduce.5.cloned.1.call-update) | async-done | bytes 262160 | tf_op jit(solution)/shard_map/while/body/eval_jaxpr/psum | solution.py:186
  1112.6 2.1 select_select_fusion.15
  1118.0 3.9 collective-permute-done.1
  1121.9 3.3 copy.27
  1125.2 2.5 convert_bitcast_fusion
  1127.7 2.3 pad_maximum_fusion
  1130.1 233.8 %reduce-scatter.2.cloned.1.call-done = bf16[32,2,1024]{2,0,1:T(8,128)(2,1)} async-done(((bf16[1024,2,1024]{2,0,1:T(8,128)(2,1)}), bf16[32,2,1024]{2,0,1:T(8,128)(2,1)}) %reduce-scatter.2.cloned.1.call-update) | async-done | bytes 131088 | tf_op jit(solution)/shard_map/reduce_scatter | solution.py:206
  (296 shorter events, 151.7 us)
Async XLA Ops:
  7.2 180.2 %copy-start.9 = (f32[1,1024]{1,0:T(1,128)S(1)}, f32[1,1024]{1,0:T(1,128)}, u32[]{:S(2)}) copy-start(f32[1,1024]{1,0:T(1,128)} %param.25) | copy-start | bytes 12292
  7.2 180.2 %copy-start.7 = (f32[1,1024]{1,0:T(1,128)S(1)}, f32[1,1024]{1,0:T(1,128)}, u32[]{:S(2)}) copy-start(f32[1,1024]{1,0:T(1,128)} %param.26) | copy-start | bytes 12292
  7.2 180.2 %copy-start.6 = (f32[1,1024]{1,0:T(1,128)S(1)}, f32[1,1024]{1,0:T(1,128)}, u32[]{:S(2)}) copy-start(f32[1,1024]{1,0:T(1,128)} %param.27) | copy-start | bytes 12292
  7.2 180.2 %copy-start.8 = (f32[1,1024]{1,0:T(1,128)S(1)}, f32[1,1024]{1,0:T(1,128)}, u32[]{:S(2)}) copy-start(f32[1,1024]{1,0:T(1,128)} %param.28) | copy-start | bytes 12292
  7.2 94.7 %all-gather.5.cloned.1.call-start = ((), (), s32[]{:S(2)}) async-start(), calls=%async_computation.2 | async-start | bytes 2162688 | tf_op jit(solution)/shard_map/all_gather | solution.py:97
  7.9 179.4 %all-gather.3.cloned.1.call-start = ((), (), s32[]{:S(2)}) async-start(), calls=%async_computation.1 | async-start | bytes 2162688 | tf_op jit(solution)/shard_map/all_gather | solution.py:96
  187.5 41.5 %all-reduce.3.cloned.1.call-start = ((), (), s32[]{:S(2)}) async-start(), calls=%async_computation.4 | async-start | bytes 524288 | tf_op jit(solution)/shard_map/while/body/eval_jaxpr/psum | solution.py:139
  230.5 7.7 collective-permute-start
  238.1 44.0 %all-reduce.3.cloned.1.call-start = ((), (), s32[]{:S(2)}) async-start(), calls=%async_computation.4 | async-start | bytes 524288 | tf_op jit(solution)/shard_map/while/body/eval_jaxpr/psum | solution.py:139
  283.6 7.7 collective-permute-start
  291.3 45.7 %all-reduce.3.cloned.1.call-start = ((), (), s32[]{:S(2)}) async-start(), calls=%async_computation.4 | async-start | bytes 524288 | tf_op jit(solution)/shard_map/while/body/eval_jaxpr/psum | solution.py:139
  338.5 7.7 collective-permute-start
  346.2 44.9 %all-reduce.3.cloned.1.call-start = ((), (), s32[]{:S(2)}) async-start(), calls=%async_computation.4 | async-start | bytes 524288 | tf_op jit(solution)/shard_map/while/body/eval_jaxpr/psum | solution.py:139
  392.5 7.7 collective-permute-start
  400.2 47.2 %all-reduce.3.cloned.1.call-start = ((), (), s32[]{:S(2)}) async-start(), calls=%async_computation.4 | async-start | bytes 524288 | tf_op jit(solution)/shard_map/while/body/eval_jaxpr/psum | solution.py:139
  448.9 7.7 collective-permute-start
  456.6 46.1 %all-reduce.3.cloned.1.call-start = ((), (), s32[]{:S(2)}) async-start(), calls=%async_computation.4 | async-start | bytes 524288 | tf_op jit(solution)/shard_map/while/body/eval_jaxpr/psum | solution.py:139
  504.2 7.7 collective-permute-start
  511.9 46.9 %all-reduce.3.cloned.1.call-start = ((), (), s32[]{:S(2)}) async-start(), calls=%async_computation.4 | async-start | bytes 524288 | tf_op jit(solution)/shard_map/while/body/eval_jaxpr/psum | solution.py:139
  560.3 7.7 collective-permute-start
  568.0 44.0 %all-reduce.3.cloned.1.call-start = ((), (), s32[]{:S(2)}) async-start(), calls=%async_computation.4 | async-start | bytes 524288 | tf_op jit(solution)/shard_map/while/body/eval_jaxpr/psum | solution.py:139
  613.5 7.7 collective-permute-start
  621.2 1.3 copy-start.3
  622.5 5.0 copy-start
  622.5 5.0 copy-start.4
  627.5 49.8 %all-reduce.5.cloned.1.call-start = ((), (), s32[]{:S(2)}) async-start(), calls=%async_computation.5 | async-start | bytes 524288 | tf_op jit(solution)/shard_map/while/body/eval_jaxpr/psum | solution.py:186
  627.7 0.7 copy-start.5
  681.8 5.8 collective-permute-start.1
  687.6 52.3 %all-reduce.5.cloned.1.call-start = ((), (), s32[]{:S(2)}) async-start(), calls=%async_computation.5 | async-start | bytes 524288 | tf_op jit(solution)/shard_map/while/body/eval_jaxpr/psum | solution.py:186
  690.2 5.9 copy-start.1
  697.0 2.0 copy-start.2
  698.9 0.7 copy-start.5
  744.5 5.8 collective-permute-start.1
  750.3 53.7 %all-reduce.5.cloned.1.call-start = ((), (), s32[]{:S(2)}) async-start(), calls=%async_computation.5 | async-start | bytes 524288 | tf_op jit(solution)/shard_map/while/body/eval_jaxpr/psum | solution.py:186
  750.4 0.7 copy-start.5
  808.6 5.8 collective-permute-start.1
  814.4 52.6 %all-reduce.5.cloned.1.call-start = ((), (), s32[]{:S(2)}) async-start(), calls=%async_computation.5 | async-start | bytes 524288 | tf_op jit(solution)/shard_map/while/body/eval_jaxpr/psum | solution.py:186
  814.5 0.7 copy-start.5
  871.6 5.8 collective-permute-start.1
  877.4 52.5 %all-reduce.5.cloned.1.call-start = ((), (), s32[]{:S(2)}) async-start(), calls=%async_computation.5 | async-start | bytes 524288 | tf_op jit(solution)/shard_map/while/body/eval_jaxpr/psum | solution.py:186
  877.5 0.7 copy-start.5
  934.5 5.8 collective-permute-start.1
  940.3 51.1 %all-reduce.5.cloned.1.call-start = ((), (), s32[]{:S(2)}) async-start(), calls=%async_computation.5 | async-start | bytes 524288 | tf_op jit(solution)/shard_map/while/body/eval_jaxpr/psum | solution.py:186
  940.4 0.7 copy-start.5
  995.9 5.8 collective-permute-start.1
  1001.7 51.5 %all-reduce.5.cloned.1.call-start = ((), (), s32[]{:S(2)}) async-start(), calls=%async_computation.5 | async-start | bytes 524288 | tf_op jit(solution)/shard_map/while/body/eval_jaxpr/psum | solution.py:186
  1001.8 0.7 copy-start.5
  1057.9 5.8 collective-permute-start.1
  1063.7 47.8 %all-reduce.5.cloned.1.call-start = ((), (), s32[]{:S(2)}) async-start(), calls=%async_computation.5 | async-start | bytes 524288 | tf_op jit(solution)/shard_map/while/body/eval_jaxpr/psum | solution.py:186
  1063.8 0.7 copy-start.5
  1116.1 5.8 collective-permute-start.1
  1121.9 242.0 %reduce-scatter.2.cloned.1.call-start = ((), (), s32[]{:S(2)}) async-start(), calls=%async_computation.3 | async-start | bytes 4325376 | tf_op jit(solution)/shard_map/reduce_scatter | solution.py:206
Sparse Core Ops, SparseCore 0:
  11.2 90.6 all-gather.4
  105.1 82.2 all-gather.2
  191.4 37.5 all-reduce.2
  241.8 40.3 all-reduce.2
  295.0 42.0 all-reduce.2
  349.8 41.1 all-reduce.2
  404.2 43.2 all-reduce.2
  460.6 42.0 all-reduce.2
  518.7 40.0 all-reduce.2
  571.6 40.3 all-reduce.2
  631.2 46.0 all-reduce.4
  699.8 40.0 all-reduce.4
  754.0 49.9 all-reduce.4
  817.8 49.1 all-reduce.4
  880.8 49.0 all-reduce.4
  943.6 47.6 all-reduce.4
  1005.1 48.1 all-reduce.4
  1067.0 44.3 all-reduce.4
  1130.2 233.6 reduce-scatter.1
where the time goes:
time: 1370 us
  waiting for transfers between devices  1160 us (85%)
  other arithmetic  106 us (8%)
  local copies, waits for them, and re-layouts  44.2 us (3%)
  starting transfers between devices  30.9 us (2%)
  between operations  14.6 us (1%)
    psum x8, waiting for transfers between devices, backward_step(): lax.psum(partial_value.astype(jnp.bfloat16), 'tensor').astype(jnp.float32)  390 us
    psum x8, waiting for transfers between devices, forward_step(): lax.psum(partial_value.astype(jnp.bfloat16), 'tensor').astype(jnp.float32)  316 us
    reduce_scatter x1, waiting for transfers between devices, per_device(): lax.psum_scatter(share_terms((accum_up, accum_down)).astype(jnp.bfloat16)...  234 us
    all_gather x1, waiting for transfers between devices, per_device(): lax.all_gather(w_down, 'dp', axis=2, tiled=True)  89.1 us
    all_gather x1, waiting for transfers between devices, per_device(): lax.all_gather(w_up, 'dp', axis=1, tiled=True)  82.6 us
    select_n x40, other arithmetic, place(): return jnp.where(active, fresh, buffer)  60.9 us
    ppermute x16, waiting for transfers between devices, passed_along(): return lax.ppermute(block, axis, route)  48.4 us
    ppermute x16, starting transfers between devices, passed_along(): return lax.ppermute(block, axis, route)  30.7 us
  transfers between devices with their start and end apart: 35, of which 35 were waited for; matrix products, arithmetic and copies ran while one was open for 4% of the time, Pallas kernels for 0%

commit v1 on v0

v1 whole, which is shorter than its diff:
```python
import functools

import jax
import jax.numpy as jnp
from jax import lax
from jax.experimental import pallas as pl
from jax.experimental.pallas import tpu as pltpu
from jax.sharding import PartitionSpec as P

MESH = pl.DeviceIdType.MESH
BF16 = jnp.bfloat16
F32 = jnp.float32
Y_LO = 2
Y_HI = 4

root_half = 0.7071067811865476
density = 0.3989422804014327
epsilon = 1e-05


class Place:
    def __init__(self, n_dp, y_hi=Y_HI):
        self.y_hi_n = y_hi
        self.z_n = n_dp // y_hi
        self.y_n = y_hi * Y_LO
        self.dp = lax.axis_index("dp")
        self.lo = lax.axis_index("tensor")
        self.hi = self.dp // self.z_n
        self.z = self.dp % self.z_n
        self.y = self.hi * Y_LO + self.lo

    def at_y(self, y):
        return {"dp": (y // Y_LO) * self.z_n + self.z, "tensor": y % Y_LO}

    def at_z(self, z):
        return {"dp": self.hi * self.z_n + z, "tensor": self.lo}

    def step_y(self, d):
        return (self.y + d + self.y_n) % self.y_n

    def step_z(self, d):
        return (self.z + d + self.z_n) % self.z_n


def signal(barrier, device_id):
    pl.semaphore_signal(barrier, inc=1, device_id=device_id, device_id_type=MESH)


def remote(src, dst, send_sem, recv_sem, device_id):
    return pltpu.make_async_remote_copy(
        src_ref=src, dst_ref=dst, send_sem=send_sem, recv_sem=recv_sem, device_id=device_id, device_id_type=MESH
    )


class Ring:
    def __init__(self, n, step, slot, device, send_sem, recv_sem):
        self.n, self.step, self.slot, self.device = n, step, slot, device
        self.send_sem, self.recv_sem = send_sem, recv_sem
        self.rounds = n // 2
        self.copies = {}

    def start(self, r):
        last = r == self.rounds - 1
        for way, sign in ((0, 1), (1, -1)):
            block = self.slot(self.step(-sign * r), way if last else None)
            copy = remote(
                block, block, self.send_sem.at[way, r], self.recv_sem.at[way, r], self.device(self.step(sign))
            )
            copy.start()
            self.copies[way, r] = copy

    def wait_recv(self, r):
        last = r == self.rounds - 1
        for way, sign in ((0, 1), (1, -1)):
            block = self.slot(self.step(-sign * (r + 1)), way if last else None)
            remote(
                block, block, self.send_sem.at[way, r], self.recv_sem.at[way, r], self.device(self.step(sign))
            ).wait_recv()

    def wait_send(self):
        for copy in self.copies.values():
            copy.wait_send()


def run_rings(rings):
    for r in range(max(ring.rounds for ring in rings)):
        live = [ring for ring in rings if r < ring.rounds]
        for ring in live:
            ring.start(r)
        for ring in live:
            ring.wait_recv(r)


def half_of(ref, part, size):
    return ref if part is None else ref.at[pl.ds(part * (size // 2), size // 2)]


def gather_kernel(
    n_dp, y_hi, up_ref, down_ref, bias_ref, up_all, down_all, bias_all, send_sem, recv_sem, bias_sem
):
    at = Place(n_dp, y_hi)
    rows = up_ref.shape[0]
    peer = {"tensor": 1 - at.lo}
    barrier = pltpu.get_barrier_semaphore()
    for d in (1, -1):
        signal(barrier, at.at_y(at.step_y(d)))
        signal(barrier, at.at_z(at.step_z(d)))
    up_all[at.lo, at.hi, at.z] = up_ref[...]
    down_all[at.lo, at.hi, at.z] = down_ref[...]
    bias_all[at.lo] = bias_ref[...]
    pl.semaphore_wait(barrier, 4)

    bias_copy = remote(bias_all.at[at.lo], bias_all.at[at.lo], bias_sem.at[0], bias_sem.at[1], peer)
    bias_copy.start()

    def up_block(y, part):
        return half_of(up_all.at[y % Y_LO, y // Y_LO, at.z], part, rows)

    def down_block(z, part):
        return half_of(down_all.at[at.lo, at.hi, z], part, rows)

    def up_column(z, part):
        if part is None:
            return up_all.at[:, :, z]
        return up_all.at[part, :, z]

    def down_row(y, part):
        return half_of(down_all.at[y % Y_LO, y // Y_LO], part, at.z_n)

    first = [
        Ring(at.y_n, at.step_y, up_block, at.at_y, send_sem.at[0], recv_sem.at[0]),
        Ring(at.z_n, at.step_z, down_block, at.at_z, send_sem.at[1], recv_sem.at[1]),
    ]
    run_rings(first)
    second = [
        Ring(at.z_n, at.step_z, up_column, at.at_z, send_sem.at[2], recv_sem.at[2]),
        Ring(at.y_n, at.step_y, down_row, at.at_y, send_sem.at[3], recv_sem.at[3]),
    ]
    run_rings(second)
    for ring in first + second:
        ring.wait_send()
    remote(
        bias_all.at[1 - at.lo], bias_all.at[1 - at.lo], bias_sem.at[0], bias_sem.at[1], peer
    ).wait_recv()
    bias_copy.wait_send()


def gelu_value(pre_gelu):
    return pre_gelu * 0.5 * (1.0 + lax.erf(pre_gelu * root_half))


def gelu_slope(pre_gelu):
    return (
        0.5 * (1.0 + lax.erf(pre_gelu * root_half))
        + pre_gelu * jnp.exp(-0.5 * pre_gelu * pre_gelu) * density
    )


def outer_t(left, right):
    return lax.dot_general(left, right, (((1,), (1,)), ((), ())), preferred_element_type=F32)


def inner(left, right):
    return lax.dot_general(left, right, (((0,), (0,)), ((), ())), preferred_element_type=F32)


def coded(values, base, bound):
    base = base.astype(F32)
    return (base + jnp.clip(values.astype(F32) - base, -bound, bound)).astype(BF16)


def chain_kernel(
    n_sections,
    tile,
    sid_ref,
    emb_ref,
    cot_ref,
    fst_ref,
    bst_ref,
    fsc_ref,
    bsc_ref,
    gain_ref,
    bias_ref,
    bdown_ref,
    bup_ref,
    wu_ref,
    wd_ref,
    out_ref,
    ig_ref,
    normed_ref,
    act_ref,
    pg_ref,
    g_ref,
    x_in,
    code_f,
    code_b,
    bound_f,
    bound_b,
    slope,
    unit,
    inv,
    scaled,
    fwd_send,
    fwd_recv,
    bwd_send,
    bwd_recv,
    peer_send,
    peer_recv,
):
    section = lax.axis_index("section")
    lo = lax.axis_index("tensor")
    rows, width = x_in.shape
    half = wu_ref.shape[2]
    tiles = half // tile
    wide = min(width, 256)
    d_tiles = width // wide
    mine = pl.ds(pl.multiple_of(lo * rows, rows), rows)
    not_first = section > 0
    not_last = section < n_sections - 1
    after = {"section": jnp.minimum(section + 1, n_sections - 1)}
    before = {"section": jnp.maximum(section - 1, 0)}
    peer = {"tensor": 1 - lo}

    barrier = pltpu.get_barrier_semaphore()
    signal(barrier, peer)

    @pl.when(not_first)
    def _():
        signal(barrier, before)

    @pl.when(not_last)
    def _():
        signal(barrier, after)

    sid = sid_ref[0]
    block = width // fsc_ref.shape[1]
    for b in range(fsc_ref.shape[1]):
        cols = pl.ds(b * block, block)
        bound_f[:, cols] = jnp.broadcast_to(0.25 * fsc_ref[mine, b : b + 1].astype(F32), (rows, block))
        bound_b[:, cols] = jnp.broadcast_to(0.25 * bsc_ref[mine, b : b + 1].astype(F32), (rows, block))

    @pl.when(section == 0)
    def _():
        x_in[...] = emb_ref[mine, :]

    @pl.when(jnp.logical_not(not_last))
    def _():
        g_ref[...] = cot_ref[mine, :]

    pl.semaphore_wait(barrier, 1 + not_first.astype(jnp.int32) + not_last.astype(jnp.int32))

    def columns(j):
        return pl.ds(pl.multiple_of(j * wide, wide), wide)

    def fwd_copy(j):
        return remote(code_f.at[:, columns(j)], x_in.at[:, columns(j)], fwd_send.at[j], fwd_recv.at[j], after)

    def bwd_copy(j):
        return remote(code_b.at[:, columns(j)], g_ref.at[:, columns(j)], bwd_send.at[j], bwd_recv.at[j], before)

    @pl.when(not_first)
    def _():
        for j in range(d_tiles):
            fwd_copy(j).wait_recv()

    values = x_in[...].astype(F32)
    centered = values - jnp.mean(values, axis=-1, keepdims=True)
    inverse = lax.rsqrt(jnp.mean(centered * centered, axis=-1, keepdims=True) + epsilon)
    unit_values = centered * inverse
    normed_ref[...] = (unit_values * gain_ref[...] + bias_ref[...]).astype(BF16)
    unit[...] = unit_values
    inv[...] = jnp.broadcast_to(inverse, inv.shape)

    def up_tile(j, _):
        h, c = j // tiles, j % tiles
        cols = pl.ds(pl.multiple_of(c * tile, tile), tile)
        spot = pl.ds(pl.multiple_of(j * tile, tile), tile)
        pre = jnp.dot(normed_ref[...], wu_ref[h, :, cols], preferred_element_type=F32) + bup_ref[h, 0:1, cols]
        slope[:, spot] = pre
        act_ref[:, spot] = gelu_value(pre).astype(BF16)
        return 0

    lax.fori_loop(0, 2 * tiles, up_tile, 0)

    def down_tile(j, _):
        cols = columns(j)
        total = outer_t(act_ref[:, :half], wd_ref[0, cols, :]) + outer_t(act_ref[:, half:], wd_ref[1, cols, :])
        output = (x_in[:, cols].astype(F32) + total + bdown_ref[:, cols]).astype(BF16)
        out_ref[mine, cols] = output
        code_f[:, cols] = coded(output, fst_ref[sid, mine, cols], bound_f[:, cols])

        @pl.when(not_last)
        def _():
            fwd_copy(j).start()

        return 0

    lax.fori_loop(0, d_tiles, down_tile, 0)
    out_copy = remote(out_ref.at[mine], out_ref.at[mine], peer_send.at[0], peer_recv.at[0], peer)
    out_copy.start()

    def slope_tile(j, _):
        spot = pl.ds(pl.multiple_of(j * tile, tile), tile)
        slope[:, spot] = gelu_slope(slope[:, spot])
        return 0

    lax.fori_loop(0, 2 * tiles, slope_tile, 0)

    @pl.when(not_last)
    def _():
        for j in range(d_tiles):
            fwd_copy(j).wait_send()
        for j in range(d_tiles):
            bwd_copy(j).wait_recv()

    def up_grad_tile(j, _):
        h, c = j // tiles, j % tiles
        cols = pl.ds(pl.multiple_of(c * tile, tile), tile)
        spot = pl.ds(pl.multiple_of(j * tile, tile), tile)
        act_grad = jnp.dot(g_ref[...], wd_ref[h, :, cols], preferred_element_type=F32)
        pg_ref[:, spot] = (act_grad * slope[:, spot]).astype(BF16)
        return 0

    lax.fori_loop(0, 2 * tiles, up_grad_tile, 0)

    def norm_grad_tile(j, _):
        cols = columns(j)
        total = outer_t(pg_ref[:, :half], wu_ref[0, cols, :]) + outer_t(pg_ref[:, half:], wu_ref[1, cols, :])
        scaled[:, cols] = total * gain_ref[:, cols]
        return 0

    lax.fori_loop(0, d_tiles, norm_grad_tile, 0)
    scaled_values = scaled[...]
    unit_values = unit[...]
    first_mean = jnp.mean(scaled_values, axis=-1, keepdims=True)
    second_mean = jnp.mean(scaled_values * unit_values, axis=-1, keepdims=True)

    for j in range(d_tiles):
        cols = columns(j)
        inner_part = scaled[:, cols] - first_mean - unit[:, cols] * second_mean
        input_grad = (g_ref[:, cols].astype(F32) + inv[:, 0:1] * inner_part).astype(BF16)
        ig_ref[mine, cols] = input_grad
        code_b[:, cols] = coded(input_grad, bst_ref[sid, mine, cols], bound_b[:, cols])

        @pl.when(not_first)
        def _():
            bwd_copy(j).start()

    ig_copy = remote(ig_ref.at[mine], ig_ref.at[mine], peer_send.at[1], peer_recv.at[1], peer)
    ig_copy.start()

    @pl.when(not_first)
    def _():
        for j in range(d_tiles):
            bwd_copy(j).wait_send()

    other = pl.ds(pl.multiple_of((1 - lo) * rows, rows), rows)
    remote(out_ref.at[other], out_ref.at[other], peer_send.at[0], peer_recv.at[0], peer).wait_recv()
    remote(ig_ref.at[other], ig_ref.at[other], peer_send.at[1], peer_recv.at[1], peer).wait_recv()
    out_copy.wait_send()
    ig_copy.wait_send()


def grads_kernel(
    n_dp,
    y_hi,
    normed_ref,
    act_ref,
    pg_ref,
    g_ref,
    up_out,
    down_out,
    normed_all,
    act_all,
    pg_all,
    g_all,
    up_block,
    down_block,
    ex_send,
    ex_recv,
    ring_send,
    ring_recv,
    out_send,
    out_recv,
):
    at = Place(n_dp, y_hi)
    rows = normed_ref.shape[0]
    features = normed_all.shape[3]
    hidden = act_all.shape[3]
    out_rows = up_out.shape[0]
    owner_z = at.dp // at.y_hi_n

    barrier = pltpu.get_barrier_semaphore()
    for d in range(1, at.y_n):
        signal(barrier, at.at_y(at.step_y(d)))
    for d in range(1, at.z_n):
        signal(barrier, at.at_z(at.step_z(d)))
    for i in range(at.y_hi_n):
        source = i * at.z_n + owner_z
        target = at.z * at.y_hi_n + i

        @pl.when(source != at.dp)
        def _():
            signal(barrier, {"dp": source})

    sends_self = jnp.int32(0)
    for i in range(at.y_hi_n):
        sends_self = sends_self + (at.z * at.y_hi_n + i == at.dp).astype(jnp.int32)
    pl.semaphore_wait(barrier, at.y_n + at.z_n - 2 + at.y_hi_n - sends_self)

    def feature_cols(z):
        return pl.ds(pl.multiple_of(z * features, features), features)

    def hidden_cols(y):
        spot = (y % Y_LO) * at.y_hi_n + y // Y_LO
        return pl.ds(pl.multiple_of(spot * hidden, hidden), hidden)

    def z_copy(k, src, dst, d):
        target = at.step_z(d)
        return remote(
            src.at[:, feature_cols(target)], dst.at[at.y, at.z], ex_send.at[k, d], ex_recv.at[k, d], at.at_z(target)
        )

    def y_copy(k, src, dst, d):
        target = at.step_y(d)
        return remote(
            src.at[:, hidden_cols(target)], dst.at[at.y, at.z], ex_send.at[k, d], ex_recv.at[k, d], at.at_y(target)
        )

    z_parts = ((0, normed_ref, normed_all), (1, g_ref, g_all))
    y_parts = ((2, act_ref, act_all), (3, pg_ref, pg_all))
    for d in range(1, at.y_n):
        for k, src, dst in y_parts:
            y_copy(k, src, dst, d).start()
    for d in range(1, at.z_n):
        for k, src, dst in z_parts:
            z_copy(k, src, dst, d).start()
    for k, src, dst in z_parts:
        dst[at.y, at.z] = src[:, feature_cols(at.z)]
    for k, src, dst in y_parts:
        dst[at.y, at.z] = src[:, hidden_cols(at.y)]
    for d in range(1, at.y_n):
        for k, src, dst in y_parts:
            spot = dst.at[at.step_y(-d), at.z]
            remote(spot, spot, ex_send.at[k, d], ex_recv.at[k, d], at.at_y(at.step_y(d))).wait_recv()
    for d in range(1, at.z_n):
        for k, src, dst in z_parts:
            spot = dst.at[at.y, at.step_z(-d)]
            remote(spot, spot, ex_send.at[k, d], ex_recv.at[k, d], at.at_z(at.step_z(d))).wait_recv()

    def row_slot(ref):
        return lambda y, part: half_of(ref.at[y], part, at.z_n)

    def column_slot(ref):
        half = at.y_n // 2

        def slot(z, part):
            if part is None:
                return ref.at[:, z]
            return ref.at[pl.ds(part * half, half), z]

        return slot

    rings = [
        Ring(at.z_n, at.step_z, column_slot(pg_all), at.at_z, ring_send.at[3], ring_recv.at[3]),
        Ring(at.z_n, at.step_z, column_slot(act_all), at.at_z, ring_send.at[2], ring_recv.at[2]),
        Ring(at.y_n, at.step_y, row_slot(normed_all), at.at_y, ring_send.at[0], ring_recv.at[0]),
        Ring(at.y_n, at.step_y, row_slot(g_all), at.at_y, ring_send.at[1], ring_recv.at[1]),
    ]
    run_rings(rings)

    tokens = at.z_n * rows

    def accumulate(block, left, right):
        block[...] = jnp.zeros_like(block)

        def body(y, _):
            block[...] += inner(left[y].reshape(tokens, features), right[y].reshape(tokens, hidden))
            return 0

        lax.fori_loop(0, at.y_n, body, 0)

    accumulate(up_block, normed_all, pg_all)
    accumulate(down_block, g_all, act_all)

    out_cols = pl.ds(pl.multiple_of(at.hi * hidden, hidden), hidden)

    def out_copy(k, block, out, i):
        return remote(
            block.at[pl.ds(i * out_rows, out_rows)],
            out.at[:, out_cols],
            out_send.at[k, i],
            out_recv.at[k, at.hi],
            {"dp": at.z * at.y_hi_n + i},
        )

    outs = ((0, up_block, up_out), (1, down_block, down_out))
    for i in range(at.y_hi_n):
        own = at.z * at.y_hi_n + i == at.dp

        @pl.when(jnp.logical_not(own))
        def _():
            for k, block, out in outs:
                out_copy(k, block, out, i).start()

        @pl.when(own)
        def _():
            for k, block, out in outs:
                out[:, out_cols] = block[pl.ds(i * out_rows, out_rows), :]

    for i in range(at.y_hi_n):

        @pl.when(i * at.z_n + owner_z != at.dp)
        def _():
            for k, block, out in outs:
                spot = out.at[:, pl.ds(i * hidden, hidden)]
                remote(spot, spot, out_send.at[k, 0], out_recv.at[k, i], {"dp": at.z * at.y_hi_n + i}).wait_recv()

    for i in range(at.y_hi_n):

        @pl.when(at.z * at.y_hi_n + i != at.dp)
        def _():
            for k, block, out in outs:
                out_copy(k, block, out, i).wait_send()

    for d in range(1, at.y_n):
        for k, src, dst in y_parts:
            y_copy(k, src, dst, d).wait_send()
    for d in range(1, at.z_n):
        for k, src, dst in z_parts:
            z_copy(k, src, dst, d).wait_send()
    for ring in rings:
        ring.wait_send()


def vmem(count):
    return [pl.BlockSpec(memory_space=pltpu.VMEM)] * count


def params(collective_id, limit=56):
    return pltpu.CompilerParams(
        collective_id=collective_id, has_side_effects=True, vmem_limit_bytes=limit * 1024 * 1024
    )


def per_device(
    n_sections,
    n_dp,
    y_hi,
    embeddings,
    cotangent,
    w_up,
    w_down,
    b_up,
    b_down,
    ln_gain,
    ln_bias,
    fwd_store,
    bwd_store,
    sample_ids,
    fwd_scales,
    bwd_scales,
):
    z_n = n_dp // y_hi
    y_n = y_hi * Y_LO
    shard, half = w_up.shape[1:]
    width = embeddings.shape[1]
    rows = embeddings.shape[0] // Y_LO
    dma = pltpu.SemaphoreType.DMA
    rounds = max(y_n, z_n) // 2
    whole = jax.ShapeDtypeStruct((Y_LO, y_hi, z_n, shard, half), BF16)
    up_all, down_all, bias_all = pl.pallas_call(
        functools.partial(gather_kernel, n_dp, y_hi),
        out_shape=(whole, whole, jax.ShapeDtypeStruct((Y_LO, 8, half), F32)),
        in_specs=vmem(3),
        out_specs=tuple(vmem(3)),
        scratch_shapes=[dma((4, 2, rounds)), dma((4, 2, rounds)), dma((2,))],
        compiler_params=params(0),
    )(w_up[0], w_down[0].T, jnp.broadcast_to(b_up, (8, half)))
    up_all = up_all.reshape(Y_LO, width, half)
    down_all = down_all.reshape(Y_LO, width, half)

    d_tiles = width // min(width, 256)
    hidden_all = Y_LO * half
    out, ig, normed, act, pre_grad, upstream = pl.pallas_call(
        functools.partial(chain_kernel, n_sections, min(half, 512)),
        out_shape=(
            jax.ShapeDtypeStruct(embeddings.shape, BF16),
            jax.ShapeDtypeStruct(embeddings.shape, BF16),
            jax.ShapeDtypeStruct((rows, width), BF16),
            jax.ShapeDtypeStruct((rows, hidden_all), BF16),
            jax.ShapeDtypeStruct((rows, hidden_all), BF16),
            jax.ShapeDtypeStruct((rows, width), BF16),
        ),
        in_specs=[pl.BlockSpec(memory_space=pltpu.SMEM)] + vmem(12),
        out_specs=tuple(vmem(6)),
        scratch_shapes=[
            pltpu.VMEM((rows, width), BF16),
            pltpu.VMEM((rows, width), BF16),
            pltpu.VMEM((rows, width), BF16),
            pltpu.VMEM((rows, width), F32),
            pltpu.VMEM((rows, width), F32),
            pltpu.VMEM((rows, hidden_all), F32),
            pltpu.VMEM((rows, width), F32),
            pltpu.VMEM((rows, 128), F32),
            pltpu.VMEM((rows, width), F32),
            dma((d_tiles,)),
            dma((d_tiles,)),
            dma((d_tiles,)),
            dma((d_tiles,)),
            dma((2,)),
            dma((2,)),
        ],
        compiler_params=params(1),
    )(
        sample_ids,
        embeddings,
        cotangent,
        fwd_store[0],
        bwd_store[0],
        fwd_scales[0],
        bwd_scales[0],
        ln_gain,
        ln_bias,
        b_down,
        bias_all,
        up_all,
        down_all,
    )

    features = width // z_n
    hidden = hidden_all // y_n
    peers = max(y_n, z_n)
    grad_up, grad_down = pl.pallas_call(
        functools.partial(grads_kernel, n_dp, y_hi),
        out_shape=(jax.ShapeDtypeStruct((shard, half), F32), jax.ShapeDtypeStruct((shard, half), F32)),
        in_specs=vmem(4),
        out_specs=tuple(vmem(2)),
        scratch_shapes=[
            pltpu.VMEM((y_n, z_n, rows, features), BF16),
            pltpu.VMEM((y_n, z_n, rows, hidden), BF16),
            pltpu.VMEM((y_n, z_n, rows, hidden), BF16),
            pltpu.VMEM((y_n, z_n, rows, features), BF16),
            pltpu.VMEM((features, hidden), F32),
            pltpu.VMEM((features, hidden), F32),
            dma((4, peers)),
            dma((4, peers)),
            dma((4, 2, rounds)),
            dma((4, 2, rounds)),
            dma((2, y_hi)),
            dma((2, y_hi)),
        ],
        compiler_params=params(2),
    )(normed, act, pre_grad, upstream)
    return (out[None], ig[None], grad_up[None], grad_down[None])


def solution(mesh, y_hi=Y_HI):
    return jax.shard_map(
        functools.partial(per_device, mesh.shape["section"], mesh.shape["dp"], y_hi),
        mesh=mesh,
        in_specs=(
            P("dp", None),
            P("dp", None),
            P("section", "dp", "tensor"),
            P("section", "tensor", "dp"),
            P("section", "tensor"),
            P("section", None),
            P("section", None),
            P("section", None),
            P("section", "dp", None, None),
            P("section", "dp", None, None),
            P("dp"),
            P("section", "dp", None),
            P("section", "dp", None),
        ),
        out_specs=(
            P("section", "dp", None),
            P("section", "dp", None),
            P("section", "dp", "tensor"),
            P("section", "dp", "tensor"),
        ),
        check_vma=False,
    )
```

time: 1370 us -> 259 us (0.19)
  the two profiles are of different devices: /device:TPU:6 before, /device:TPU:8 now
where the time goes in v1:
time: 259 us
  Pallas kernels  247 us (95%)
  local copies, waits for them, and re-layouts  10.6 us (4%)
    pallas_call x1, Pallas kernels, per_device(): pl.pallas_call(functools.partial(chain_kernel, n_sections, min(half, 512)...  91.1 us
    pallas_call x1, Pallas kernels, per_device(): pl.pallas_call(functools.partial(grads_kernel, n_dp, y_hi), out_shape=(ja...  83.1 us
    pallas_call x1, Pallas kernels, per_device(): pl.pallas_call(functools.partial(gather_kernel, n_dp, y_hi), out_shape=(w...  72.7 us
    unnamed x6, local copies, waits for them, and re-layouts  9.3 us

profile of v1, /device:TPU:8, one launch (start us, length us, event | category | flops | bytes accessed | tf_op | source)
XLA Modules:
  0.0 258.7 jit_solution(6925755861739409496)
XLA Ops:
  1.3 1.3 broadcast_in_dim.20.bias_ref
  2.6 1.4 copy.17
  4.0 1.4 copy.18
  5.4 72.7 %shard_map.156 = (bf16[2,4,8,32,1024]{4,3,2,1,0:T(8,128)(2,1)}, bf16[2,4,8,32,1024]{4,3,2,1,0:T(8,128)(2,1)}, f32[2,8,1024]{2,1,0:T(8,128)}) custom-call(bf16[32,1024]{1,0:T(8,128)(2,1)} %bitcast.25, bf16[32,1024]{1,0:T(8,128)(2,1)} %bitcast.26, f32[8,1024]{1,0:T(8,128)} %broadcast_in_dim.20.bias_ref), custom_call_target="tpu_custom_call" | custom-call | tf_op jit(solution)/shard_map/pallas_call | solution.py:572
  78.1 91.1 %shard_map.157 = (bf16[128,1024]{1,0:T(8,128)(2,1)}, bf16[128,1024]{1,0:T(8,128)(2,1)}, bf16[64,1024]{1,0:T(8,128)(2,1)}, bf16[64,2048]{1,0:T(8,128)(2,1)}, bf16...) custom-call(s32[1]{0:T(128)S(6)} %copy.23.sid_ref, bf16[128,1024]{1,0:T(8,128)(2,1)} %emb_ref.1, ...), custom_call_target="tpu_custom_call" | custom-call | tf_op jit(solution)/shard_map/pallas_call | solution.py:585
  169.2 83.1 %shard_map.158 = (f32[32,1024]{1,0:T(8,128)}, f32[32,1024]{1,0:T(8,128)}) custom-call(bf16[64,1024]{1,0:T(8,128)(2,1)} %get-tuple-element.20.normed_ref, bf16[64,2048]{1,0:T(8,128)(2,1)} %get-tuple-element.21.act_ref, bf16[64,2048]{1,0:T(8,128)(2,1)} %get-tuple-element.22.pg_ref, bf16[64,1024]{1,0:T(8,128)(2,1)} %get-tuple-element.23.g_ref), custom_call_target="tpu_custom_call" | custom-call | tf_op jit(solution)/shard_map/pallas_call | solution.py:634
  252.3 1.7 copy.24
  253.9 1.7 copy.25
  255.6 1.6 copy.26
  257.2 1.6 copy.27

commit v2 on v0

v2 whole, which is shorter than its diff:
```python
import functools

import jax
import jax.numpy as jnp
from jax import lax
from jax.experimental import pallas as pl
from jax.experimental.pallas import tpu as pltpu
from jax.sharding import PartitionSpec as P

MESH = pl.DeviceIdType.MESH
BF16 = jnp.bfloat16
F32 = jnp.float32
Y_LO = 2
Y_HI = 4

root_half = 0.7071067811865476
density = 0.3989422804014327
epsilon = 1e-05


class Place:
    def __init__(self, n_dp, y_hi=Y_HI):
        self.y_hi_n = y_hi
        self.z_n = n_dp // y_hi
        self.y_n = y_hi * Y_LO
        self.dp = lax.axis_index("dp")
        self.lo = lax.axis_index("tensor")
        self.hi = self.dp // self.z_n
        self.z = self.dp % self.z_n
        self.y = self.hi * Y_LO + self.lo

    def at_y(self, y):
        return {"dp": (y // Y_LO) * self.z_n + self.z, "tensor": y % Y_LO}

    def at_z(self, z):
        return {"dp": self.hi * self.z_n + z, "tensor": self.lo}

    def step_y(self, d):
        return (self.y + d + self.y_n) % self.y_n

    def step_z(self, d):
        return (self.z + d + self.z_n) % self.z_n


def signal(barrier, device_id):
    pl.semaphore_signal(barrier, inc=1, device_id=device_id, device_id_type=MESH)


def remote(src, dst, send_sem, recv_sem, device_id):
    return pltpu.make_async_remote_copy(
        src_ref=src, dst_ref=dst, send_sem=send_sem, recv_sem=recv_sem, device_id=device_id, device_id_type=MESH
    )


class Ring:
    def __init__(self, n, step, slot, device, sems, index, last_way):
        self.step, self.slot, self.device = step, slot, device
        self.send_sem, self.recv_sem, self.index = sems[0], sems[1], index
        self.rounds = n // 2
        self.last_way = last_way

    def ways(self, r):
        return (self.last_way,) if r == self.rounds - 1 else (0, 1)

    def copy(self, way, r, received=False):
        sign = 1 - 2 * way
        block = self.slot(self.step(-sign * (r + 1 if received else r)))
        spot = (self.index, way, r)
        return remote(block, block, self.send_sem.at[spot], self.recv_sem.at[spot], self.device(self.step(sign)))

    def start(self, r):
        for way in self.ways(r):
            self.copy(way, r).start()

    def wait_recv(self, r):
        for way in self.ways(r):
            self.copy(way, r, True).wait_recv()

    def wait_send(self):
        for r in range(self.rounds):
            for way in self.ways(r):
                self.copy(way, r).wait_send()


def run_rings(rings, done=None):
    rounds = max(ring.rounds for ring in rings)
    for ring in rings:
        ring.start(0)
    for r in range(rounds):
        for ring in rings:
            if r < ring.rounds:
                ring.wait_recv(r)
                if r + 1 < ring.rounds:
                    ring.start(r + 1)
        if done is not None:
            done(r)


def run_gathers(pairs, lag=1.0):
    free, events, order = {}, [], []

    def push(ready, axis, ring, way, r, pair):
        begin = max(ready, free.get((axis, way), 0.0))
        free[axis, way] = begin + 1.0
        events.append((begin + 1.0 + lag, len(order) + len(events), ring, way, r, pair))
        return lambda: ring.copy(way, r).start()

    def begin_chunk(ready, pair, d):
        axis, ring = pair[2], pair[3][d]
        return [push(ready, axis, ring, way, 0, pair) for way in ring.ways(0)]

    starts = []
    for pair in pairs:
        starts += [push(0.0, pair[0], pair[1], way, 0, pair) for way in pair[1].ways(0)]
    for pair in pairs:
        starts += begin_chunk(0.0, pair, 0)
    for start in starts:
        start()
    while events:
        event = min(events, key=lambda e: e[:2])
        events.remove(event)
        order.append(event)
        now, _, ring, way, r, pair = event
        ring.copy(way, r, True).wait_recv()
        starts = []
        first = ring is pair[1]
        if r + 1 < ring.rounds and way in ring.ways(r + 1):
            starts.append(push(now, pair[0] if first else pair[2], ring, way, r + 1, pair))
        if first:
            starts += begin_chunk(now, pair, -(r + 1) if way == 0 else r + 1)
        for start in starts:
            start()


def gelu_value(pre_gelu):
    return pre_gelu * 0.5 * (1.0 + lax.erf(pre_gelu * root_half))


def gelu_slope(pre_gelu):
    return (
        0.5 * (1.0 + lax.erf(pre_gelu * root_half))
        + pre_gelu * jnp.exp(-0.5 * pre_gelu * pre_gelu) * density
    )


def outer_t(left, right):
    return lax.dot_general(left, right, (((1,), (1,)), ((), ())), preferred_element_type=F32)


def inner(left, right):
    return lax.dot_general(left, right, (((0,), (0,)), ((), ())), preferred_element_type=F32)


def coded(values, base, bound):
    base = base.astype(F32)
    return (base + jnp.clip(values.astype(F32) - base, -bound, bound)).astype(BF16)


def layer_kernel(
    n_sections,
    n_dp,
    y_hi,
    sid_ref,
    emb_ref,
    cot_ref,
    up_ref,
    down_ref,
    bup_ref,
    bdown_ref,
    gain_ref,
    bias_ref,
    fst_ref,
    bst_ref,
    fsc_ref,
    bsc_ref,
    out_ref,
    ig_ref,
    up_out,
    down_out,
    up_all,
    down_all,
    bias_all,
    x_in,
    g_in,
    fst,
    bst,
    normed,
    act,
    pre_grad,
    out_rows,
    ig_rows,
    code_f,
    code_b,
    bound_f,
    bound_b,
    slope,
    unit,
    inv,
    scaled,
    normed_all,
    act_all,
    pg_all,
    g_all,
    up_block,
    down_block,
    load_sem,
    bias_sem,
    hop_send,
    hop_recv,
    peer_send,
    peer_recv,
    ring_send,
    ring_recv,
    ex_send,
    ex_recv,
    out_send,
    out_recv,
):
    at = Place(n_dp, y_hi)
    section = lax.axis_index("section")
    rows, width = x_in.shape
    half = up_all.shape[4]
    features = normed_all.shape[3]
    hidden = act_all.shape[3]
    shard = up_ref.shape[0]
    wide = width // 2
    sems = (ring_send, ring_recv)
    mine = pl.ds(pl.multiple_of(at.lo * rows, rows), rows)
    other = pl.ds(pl.multiple_of((1 - at.lo) * rows, rows), rows)
    not_first = section > 0
    not_last = section < n_sections - 1
    early_first = section < n_sections // 2
    after = {"section": jnp.minimum(section + 1, n_sections - 1)}
    before = {"section": jnp.maximum(section - 1, 0)}
    peer = {"tensor": 1 - at.lo}
    owner_z = at.dp // at.y_hi_n

    barrier = pltpu.get_barrier_semaphore()
    for d in range(1, at.y_n):
        signal(barrier, at.at_y(at.step_y(d)))
    for d in range(1, at.z_n):
        signal(barrier, at.at_z(at.step_z(d)))
    for i in range(at.y_hi_n):
        source = i * at.z_n + owner_z

        @pl.when(source != at.dp)
        def _():
            signal(barrier, {"dp": source})

    @pl.when(not_first)
    def _():
        signal(barrier, before)

    @pl.when(not_last)
    def _():
        signal(barrier, after)

    own_up = pltpu.make_async_copy(up_ref, up_all.at[at.lo, at.hi, at.z], load_sem.at[0])
    own_down = pltpu.make_async_copy(down_ref, down_all.at[at.lo, at.hi, at.z], load_sem.at[1])
    load_fst = pltpu.make_async_copy(fst_ref.at[:, mine], fst, load_sem.at[2])
    load_bst = pltpu.make_async_copy(bst_ref.at[:, mine], bst, load_sem.at[3])
    load_emb = pltpu.make_async_copy(emb_ref.at[mine], x_in, load_sem.at[4])
    load_cot = pltpu.make_async_copy(cot_ref.at[mine], g_in, load_sem.at[5])
    own_up.start()
    own_down.start()
    load_fst.start()
    load_bst.start()

    @pl.when(section == 0)
    def _():
        load_emb.start()

    @pl.when(jnp.logical_not(not_last))
    def _():
        load_cot.start()

    bias_all[at.lo] = jnp.broadcast_to(bup_ref[...], bias_all.shape[1:])
    sends_self = jnp.int32(0)
    for i in range(at.y_hi_n):
        sends_self = sends_self + (at.z * at.y_hi_n + i == at.dp).astype(jnp.int32)
    sections_near = not_first.astype(jnp.int32) + not_last.astype(jnp.int32)
    own_up.wait()
    own_down.wait()
    pl.semaphore_wait(barrier, at.y_n + at.z_n - 2 + at.y_hi_n - sends_self + sections_near)

    bias_copy = remote(bias_all.at[at.lo], bias_all.at[at.lo], bias_sem.at[0], bias_sem.at[1], peer)
    bias_copy.start()

    def up_slot(y, z):
        return up_all.at[y % Y_LO, y // Y_LO, z]

    def down_slot(y, z):
        return down_all.at[y % Y_LO, y // Y_LO, z]

    def fixed(slot, axis, step, d):
        there = step(d)
        return (lambda z: slot(there, z)) if axis == "y" else (lambda y: slot(y, there))

    y_ring = (at.y_n, at.step_y)
    z_ring = (at.z_n, at.step_z)
    up_first = Ring(*y_ring, fixed(up_slot, "z", at.step_z, 0), at.at_y, sems, 0, 0)
    down_first = Ring(*z_ring, fixed(down_slot, "y", at.step_y, 0), at.at_z, sems, 1, 1)
    up_then, down_then = {}, {}
    index = 2
    for d in range(-(at.y_n // 2), at.y_n // 2):
        up_then[d] = Ring(*z_ring, fixed(up_slot, "y", at.step_y, d), at.at_z, sems, index, index % 2)
        index += 1
    for d in range(-(at.z_n // 2), at.z_n // 2):
        down_then[d] = Ring(*y_ring, fixed(down_slot, "z", at.step_z, d), at.at_y, sems, index, index % 2)
        index += 1
    if down_first.last_way == 1:
        down_then[at.z_n // 2] = down_then.pop(-(at.z_n // 2))
    weight_rings = [up_first, down_first, *up_then.values(), *down_then.values()]
    run_gathers((("y", up_first, "z", up_then), ("z", down_first, "y", down_then)))

    scale_f = jnp.transpose(fsc_ref[...].astype(F32))
    scale_b = jnp.transpose(bsc_ref[...].astype(F32))
    low = at.lo == 0
    scale_f = 0.25 * jnp.where(low, scale_f[:rows], scale_f[rows:])
    scale_b = 0.25 * jnp.where(low, scale_b[:rows], scale_b[rows:])
    for b in range(fsc_ref.shape[0]):
        block = width // fsc_ref.shape[0]
        cols = pl.ds(b * block, block)
        bound_f[:, cols] = jnp.broadcast_to(scale_f[:, b : b + 1], (rows, block))
        bound_b[:, cols] = jnp.broadcast_to(scale_b[:, b : b + 1], (rows, block))
    remote(bias_all.at[1 - at.lo], bias_all.at[1 - at.lo], bias_sem.at[0], bias_sem.at[1], peer).wait_recv()
    bias_copy.wait_send()
    load_fst.wait()
    load_bst.wait()
    sid = sid_ref[0]

    def columns(j):
        return pl.ds(pl.multiple_of(j * wide, wide), wide)

    def up_weights(h):
        return up_all[h].reshape(width, half)

    def down_weights(h):
        return down_all[h].reshape(width, half)

    def quarter(ref, h, j):
        count = y_hi // 2
        return ref[h, pl.ds(j * count, count)].reshape(wide, half)

    def fwd_copy(j):
        return remote(code_f.at[:, columns(j)], x_in.at[:, columns(j)], hop_send.at[0, j], hop_recv.at[0, j], after)

    def bwd_copy(j):
        return remote(code_b.at[:, columns(j)], g_in.at[:, columns(j)], hop_send.at[1, j], hop_recv.at[1, j], before)

    def hidden_half(h):
        return pl.ds(pl.multiple_of(h * half, half), half)

    def feature_cols(z):
        return pl.ds(pl.multiple_of(z * features, features), features)

    def hidden_cols(y):
        spot = (y % Y_LO) * at.y_hi_n + y // Y_LO
        return pl.ds(pl.multiple_of(spot * hidden, hidden), hidden)

    def z_copy(k, src, dst, d):
        target = at.step_z(d)
        return remote(
            src.at[:, feature_cols(target)], dst.at[at.y, at.z], ex_send.at[k, d], ex_recv.at[k, d], at.at_z(target)
        )

    def y_copy(k, src, dst, d):
        target = at.step_y(d)
        return remote(
            src.at[:, hidden_cols(target)], dst.at[at.y, at.z], ex_send.at[k, d], ex_recv.at[k, d], at.at_y(target)
        )

    def z_start(k, src, dst):
        for d in range(1, at.z_n):
            z_copy(k, src, dst, d).start()
        dst[at.y, at.z] = src[:, feature_cols(at.z)]

    def y_start(k, src, dst):
        for d in range(1, at.y_n):
            y_copy(k, src, dst, d).start()
        dst[at.y, at.z] = src[:, hidden_cols(at.y)]

    def z_wait(k, dst):
        for d in range(1, at.z_n):
            spot = dst.at[at.y, at.step_z(-d)]
            remote(spot, spot, ex_send.at[k, d], ex_recv.at[k, d], at.at_z(at.step_z(d))).wait_recv()

    def y_wait(k, dst):
        for d in range(1, at.y_n):
            spot = dst.at[at.step_y(-d), at.z]
            remote(spot, spot, ex_send.at[k, d], ex_recv.at[k, d], at.at_y(at.step_y(d))).wait_recv()

    def ex_wait_send(k, copy, src, dst, n):
        for d in range(1, n):
            copy(k, src, dst, d).wait_send()

    def row_rings(ref, first):
        part = at.z_n // 2
        return [
            Ring(*y_ring, lambda y, c=c: ref.at[y, pl.ds(c * part, part)], at.at_y, sems, first + c, c) for c in range(2)
        ]

    def column_rings(ref, first):
        part = at.y_n // 2
        return [
            Ring(*z_ring, lambda z, c=c: ref.at[pl.ds(c * part, part), z], at.at_z, sems, first + c, c) for c in range(2)
        ]

    normed_rings = row_rings(normed_all, index)
    g_rings = row_rings(g_all, index + 2)
    act_rings = column_rings(act_all, index + 4)
    pg_rings = column_rings(pg_all, index + 6)

    def early():
        y_start(2, act, act_all)
        z_start(0, normed, normed_all)
        for ring in weight_rings:
            ring.wait_send()
        y_wait(2, act_all)
        z_wait(0, normed_all)
        run_rings(act_rings + normed_rings)
        for ring in act_rings + normed_rings:
            ring.wait_send()
        ex_wait_send(0, z_copy, normed, normed_all, at.z_n)
        ex_wait_send(2, y_copy, act, act_all, at.y_n)

    @pl.when(not_first)
    def _():
        for j in range(2):
            fwd_copy(j).wait_recv()

    @pl.when(section == 0)
    def _():
        load_emb.wait()

    values = x_in[...].astype(F32)
    centered = values - jnp.mean(values, axis=-1, keepdims=True)
    inverse = lax.rsqrt(jnp.mean(centered * centered, axis=-1, keepdims=True) + epsilon)
    unit_values = centered * inverse
    normed[...] = (unit_values * gain_ref[...] + bias_ref[...]).astype(BF16)
    unit[...] = unit_values
    inv[...] = jnp.broadcast_to(inverse, inv.shape)

    def up_half(h, _):
        pre = jnp.dot(normed[...], up_weights(h), preferred_element_type=F32) + bias_all[h, 0:1, :]
        slope[:, hidden_half(h)] = pre
        act[:, hidden_half(h)] = gelu_value(pre).astype(BF16)
        return 0

    lax.fori_loop(0, 2, up_half, 0)

    def down_half(j, _):
        cols = columns(j)
        total = outer_t(act[:, :half], quarter(down_all, 0, j)) + outer_t(act[:, half:], quarter(down_all, 1, j))
        output = (x_in[:, cols].astype(F32) + total + bdown_ref[:, cols]).astype(BF16)
        out_rows[:, cols] = output
        code_f[:, cols] = coded(output, fst[sid, :, cols], bound_f[:, cols])

        @pl.when(not_last)
        def _():
            fwd_copy(j).start()

        return 0

    lax.fori_loop(0, 2, down_half, 0)
    out_keep = pltpu.make_async_copy(out_rows, out_ref.at[mine], load_sem.at[6])
    out_keep.start()
    out_copy = remote(out_rows, out_ref.at[mine], peer_send.at[0], peer_recv.at[0], peer)
    out_copy.start()

    def slope_half(h, _):
        slope[:, hidden_half(h)] = gelu_slope(slope[:, hidden_half(h)])
        return 0

    lax.fori_loop(0, 2, slope_half, 0)

    @pl.when(early_first)
    def _():
        early()

    @pl.when(not_last)
    def _():
        for j in range(2):
            bwd_copy(j).wait_recv()

    @pl.when(jnp.logical_not(not_last))
    def _():
        load_cot.wait()

    def up_grad_half(h, _):
        act_grad = jnp.dot(g_in[...], down_weights(h), preferred_element_type=F32)
        pre_grad[:, hidden_half(h)] = (act_grad * slope[:, hidden_half(h)]).astype(BF16)
        return 0

    lax.fori_loop(0, 2, up_grad_half, 0)
    y_start(3, pre_grad, pg_all)
    z_start(1, g_in, g_all)

    def norm_grad_half(j, _):
        cols = columns(j)
        total = outer_t(pre_grad[:, :half], quarter(up_all, 0, j)) + outer_t(pre_grad[:, half:], quarter(up_all, 1, j))
        scaled[:, cols] = total * gain_ref[:, cols]
        return 0

    lax.fori_loop(0, 2, norm_grad_half, 0)
    scaled_values = scaled[...]
    unit_values = unit[...]
    first_mean = jnp.mean(scaled_values, axis=-1, keepdims=True)
    second_mean = jnp.mean(scaled_values * unit_values, axis=-1, keepdims=True)

    for j in range(2):
        cols = pl.ds(j * wide, wide)
        inner_part = scaled[:, cols] - first_mean - unit[:, cols] * second_mean
        input_grad = (g_in[:, cols].astype(F32) + inv[:, 0:1] * inner_part).astype(BF16)
        ig_rows[:, cols] = input_grad
        code_b[:, cols] = coded(input_grad, bst[sid, :, cols], bound_b[:, cols])

        @pl.when(not_first)
        def _():
            bwd_copy(j).start()

    ig_keep = pltpu.make_async_copy(ig_rows, ig_ref.at[mine], load_sem.at[7])
    ig_keep.start()
    ig_copy = remote(ig_rows, ig_ref.at[mine], peer_send.at[1], peer_recv.at[1], peer)
    ig_copy.start()

    @pl.when(jnp.logical_not(early_first))
    def _():
        early()

    up_block[...] = jnp.zeros_like(up_block)
    down_block[...] = jnp.zeros_like(down_block)
    y_wait(3, pg_all)
    z_wait(1, g_all)

    def add_column(z):
        left = normed_all[:, z].reshape(at.y_n * rows, features)
        up_block[...] += inner(left, pg_all[:, z].reshape(at.y_n * rows, hidden))

    def add_row(y):
        left = g_all[y].reshape(at.z_n * rows, features)
        down_block[...] += inner(left, act_all[y].reshape(at.z_n * rows, hidden))

    def add_round(r):
        for n, step, add in ((at.z_n, at.step_z, add_column), (at.y_n, at.step_y, add_row)):
            if r + 1 < n // 2:
                lax.fori_loop(0, 2, lambda i, _, step=step, add=add: (add(step((2 * i - 1) * (r + 1))), 0)[1], 0)
            elif r + 1 == n // 2:
                add(step(r + 1))
            if r == 0:
                add(step(0))

    run_rings(pg_rings + g_rings, add_round)

    out_cols = pl.ds(pl.multiple_of(at.hi * hidden, hidden), hidden)
    outs = ((0, up_block, up_out), (1, down_block, down_out))

    def grad_copy(k, block, out, i):
        return remote(
            block.at[pl.ds(i * shard, shard)],
            out.at[:, out_cols],
            out_send.at[k, i],
            out_recv.at[k, at.hi],
            {"dp": at.z * at.y_hi_n + i},
        )

    def grad_keep(k, block, out, i):
        return pltpu.make_async_copy(block.at[pl.ds(i * shard, shard)], out.at[:, out_cols], out_send.at[k, i])

    for i in range(at.y_hi_n):
        own = at.z * at.y_hi_n + i == at.dp

        @pl.when(jnp.logical_not(own))
        def _():
            for k, block, out in outs:
                grad_copy(k, block, out, i).start()

        @pl.when(own)
        def _():
            for k, block, out in outs:
                grad_keep(k, block, out, i).start()

    @pl.when(not_last)
    def _():
        for j in range(2):
            fwd_copy(j).wait_send()

    @pl.when(not_first)
    def _():
        for j in range(2):
            bwd_copy(j).wait_send()

    ex_wait_send(1, z_copy, g_in, g_all, at.z_n)
    ex_wait_send(3, y_copy, pre_grad, pg_all, at.y_n)
    for ring in pg_rings + g_rings:
        ring.wait_send()
    remote(out_rows, out_ref.at[other], peer_send.at[0], peer_recv.at[0], peer).wait_recv()
    remote(ig_rows, ig_ref.at[other], peer_send.at[1], peer_recv.at[1], peer).wait_recv()
    out_copy.wait_send()
    ig_copy.wait_send()
    out_keep.wait()
    ig_keep.wait()

    for i in range(at.y_hi_n):

        @pl.when(i * at.z_n + owner_z != at.dp)
        def _():
            for k, block, out in outs:
                spot = out.at[:, pl.ds(i * hidden, hidden)]
                remote(spot, spot, out_send.at[k, 0], out_recv.at[k, i], {"dp": at.z * at.y_hi_n + i}).wait_recv()

    for i in range(at.y_hi_n):
        own = at.z * at.y_hi_n + i == at.dp

        @pl.when(jnp.logical_not(own))
        def _():
            for k, block, out in outs:
                grad_copy(k, block, out, i).wait_send()

        @pl.when(own)
        def _():
            for k, block, out in outs:
                grad_keep(k, block, out, i).wait()


def keep_kernel(*refs):
    count = len(refs) // 2
    sems = refs[-1]
    copies = [pltpu.make_async_copy(refs[i], refs[count + i], sems.at[i]) for i in range(count)]
    for copy in copies:
        copy.start()
    for copy in copies:
        copy.wait()


def vmem(count):
    return [pl.BlockSpec(memory_space=pltpu.VMEM)] * count


def anywhere(count):
    return [pl.BlockSpec(memory_space=pl.ANY)] * count


def per_device(
    n_sections,
    n_dp,
    y_hi,
    embeddings,
    cotangent,
    w_up,
    w_down,
    b_up,
    b_down,
    ln_gain,
    ln_bias,
    fwd_store,
    bwd_store,
    sample_ids,
    fwd_scales,
    bwd_scales,
):
    z_n = n_dp // y_hi
    y_n = y_hi * Y_LO
    shard, half = w_up.shape[1:]
    width = embeddings.shape[1]
    rows = embeddings.shape[0] // Y_LO
    hidden_all = Y_LO * half
    features = width // z_n
    hidden = hidden_all // y_n
    stored = fwd_store.shape[1]
    dma = pltpu.SemaphoreType.DMA
    rounds = max(y_n, z_n) // 2
    n_rings = 2 + y_n + z_n + 8
    peers = max(y_n, z_n)
    whole = pltpu.VMEM((Y_LO, y_hi, z_n, shard, half), BF16)
    narrow = pltpu.VMEM((rows, width), BF16)
    wide = pltpu.VMEM((rows, width), F32)
    outs = (
        jax.ShapeDtypeStruct(embeddings.shape, BF16),
        jax.ShapeDtypeStruct(embeddings.shape, BF16),
        jax.ShapeDtypeStruct((shard, half), F32),
        jax.ShapeDtypeStruct((shard, half), F32),
    )
    results = pl.pallas_call(
        functools.partial(layer_kernel, n_sections, n_dp, y_hi),
        out_shape=outs,
        in_specs=[pl.BlockSpec(memory_space=pltpu.SMEM)] + anywhere(4) + vmem(4) + anywhere(2) + vmem(2),
        out_specs=tuple(anywhere(4)),
        scratch_shapes=[
            whole,
            whole,
            pltpu.VMEM((Y_LO, 8, half), F32),
            narrow,
            narrow,
            pltpu.VMEM((stored, rows, width), BF16),
            pltpu.VMEM((stored, rows, width), BF16),
            narrow,
            pltpu.VMEM((rows, hidden_all), BF16),
            pltpu.VMEM((rows, hidden_all), BF16),
            narrow,
            narrow,
            narrow,
            narrow,
            wide,
            wide,
            pltpu.VMEM((rows, hidden_all), F32),
            wide,
            pltpu.VMEM((rows, 128), F32),
            wide,
            pltpu.VMEM((y_n, z_n, rows, features), BF16),
            pltpu.VMEM((y_n, z_n, rows, hidden), BF16),
            pltpu.VMEM((y_n, z_n, rows, hidden), BF16),
            pltpu.VMEM((y_n, z_n, rows, features), BF16),
            pltpu.VMEM((features, hidden), F32),
            pltpu.VMEM((features, hidden), F32),
            dma((8,)),
            dma((2,)),
            dma((2, 2)),
            dma((2, 2)),
            dma((2,)),
            dma((2,)),
            dma((n_rings, 2, rounds)),
            dma((n_rings, 2, rounds)),
            dma((4, peers)),
            dma((4, peers)),
            dma((2, y_hi)),
            dma((2, y_hi)),
        ],
        compiler_params=pltpu.CompilerParams(
            collective_id=0, has_side_effects=True, vmem_limit_bytes=56 * 1024 * 1024
        ),
    )(
        sample_ids,
        embeddings,
        cotangent,
        w_up[0],
        w_down[0].T,
        b_up,
        b_down,
        ln_gain,
        ln_bias,
        fwd_store[0],
        bwd_store[0],
        fwd_scales[0].T,
        bwd_scales[0].T,
    )
    kept = pl.pallas_call(
        keep_kernel,
        out_shape=outs,
        in_specs=anywhere(4),
        out_specs=tuple(anywhere(4)),
        scratch_shapes=[dma((4,))],
    )(*results)
    return tuple(array[None] for array in kept)


def solution(mesh, y_hi=Y_HI):
    return jax.shard_map(
        functools.partial(per_device, mesh.shape["section"], mesh.shape["dp"], y_hi),
        mesh=mesh,
        in_specs=(
            P("dp", None),
            P("dp", None),
            P("section", "dp", "tensor"),
            P("section", "tensor", "dp"),
            P("section", "tensor"),
            P("section", None),
            P("section", None),
            P("section", None),
            P("section", "dp", None, None),
            P("section", "dp", None, None),
            P("dp"),
            P("section", "dp", None),
            P("section", "dp", None),
        ),
        out_specs=(
            P("section", "dp", None),
            P("section", "dp", None),
            P("section", "dp", "tensor"),
            P("section", "dp", "tensor"),
        ),
        check_vma=False,
    )
```

time: 1370 us -> 224 us (0.16)
  the two profiles are of different devices: /device:TPU:6 before, /device:TPU:204 now
where the time goes in v2:
time: 224 us
  Pallas kernels  222 us (99%)
    pallas_call x1, Pallas kernels, per_device(): pl.pallas_call(functools.partial(layer_kernel, n_sections, n_dp, y_hi), o...  197 us
    pallas_call x1, Pallas kernels, per_device(): pl.pallas_call(keep_kernel, out_shape=outs, in_specs=anywhere(4), out_spe...  25 us

profile of v2, /device:TPU:204, one launch (start us, length us, event | category | flops | bytes accessed | tf_op | source)
XLA Modules:
  0.0 223.7 jit_solution(13266649340155958900)
XLA Ops:
  1.3 197.4 %shard_map.156 = (bf16[128,1024]{1,0:T(8,128)(2,1)}, bf16[128,1024]{1,0:T(8,128)(2,1)}, f32[32,1024]{1,0:T(8,128)}, f32[32,1024]{1,0:T(8,128)}) custom-call(s32[1]{0:T(128)S(6)} %copy.17.sid_ref, bf16[128,1024]{1,0:T(8,128)(2,1)} %emb_ref.1, bf16[128,1024]{1,0:T(8,128)(2,1)} %cot_ref.1, bf16[32,1024]{1,0:T(8,128)(2,1)} %bitcast.18, ...), custom_call_target="tpu_custom_call" | custom-call | tf_op jit(solution)/shard_map/pallas_call | solution.py:684
  198.7 25.0 %shard_map.157 = (bf16[128,1024]{1,0:T(8,128)(2,1)}, bf16[128,1024]{1,0:T(8,128)(2,1)}, f32[32,1024]{1,0:T(8,128)}, f32[32,1024]{1,0:T(8,128)}) custom-call(bf16[128,1024]{1,0:T(8,128)(2,1)} %get-tuple-element.12.refs_0_, bf16[128,1024]{1,0:T(8,128)(2,1)} %get-tuple-element.13.refs_1_, f32[32,1024]{1,0:T(8,128)} %get-tuple-element.14.refs_2_, ...), custom_call_target="tpu_custom_call" | custom-call | tf_op jit(solution)/shard_map/pallas_call | solution.py:747

commit v3 on v2

--- a/solution.py
+++ b/solution.py
@@ -82,54 +82,82 @@
                 self.copy(way, r).wait_send()
 
 
-def run_rings(rings, done=None):
-    rounds = max(ring.rounds for ring in rings)
-    for ring in rings:
-        ring.start(0)
-    for r in range(rounds):
-        for ring in rings:
-            if r < ring.rounds:
-                ring.wait_recv(r)
-                if r + 1 < ring.rounds:
-                    ring.start(r + 1)
-        if done is not None:
-            done(r)
+class Spread:
+    def __init__(self, n, step, part, slot, device, sems, index):
+        self.step, self.part, self.slot, self.device = step, part, slot, device
+        self.send_sem, self.recv_sem, self.index = sems[0], sems[1], index
+        self.rounds = n // 2
+
+    def ways(self, r):
+        return (0,) if r == self.rounds - 1 else (0, 1)
+
+    def copy(self, way, r, received=False):
+        sign = 1 - 2 * way
+        spot = (self.index, way, r)
+        target = self.step(sign * (r + 1))
+        block = self.slot(self.step(-sign * (r + 1) if received else 0))
+        source = block if received else self.part(target)
+        return remote(source, block, self.send_sem.at[spot], self.recv_sem.at[spot], self.device(target))
+
+    wait_send = Ring.wait_send
+
+
+def start_spreads(pairs):
+    for r in range(max(pair[1].rounds for pair in pairs)):
+        for pair in pairs:
+            if r < pair[1].rounds:
+                for way in pair[1].ways(r):
+                    pair[1].copy(way, r).start()
 
 
 def run_gathers(pairs, lag=1.0):
-    free, events, order = {}, [], []
-
-    def push(ready, axis, ring, way, r, pair):
+    free, events, count, missing, brought = {}, [], [0], {}, {}
+
+    def push(ready, axis, ring, way, r, pair, size=1.0):
         begin = max(ready, free.get((axis, way), 0.0))
-        free[axis, way] = begin + 1.0
-        events.append((begin + 1.0 + lag, len(order) + len(events), ring, way, r, pair))
-        return lambda: ring.copy(way, r).start()
+        free[axis, way] = begin + size
+        count[0] += 1
+        events.append((begin + size + lag, count[0], ring, way, r, pair))
+
+    def go(ready, axis, ring, way, r, pair):
+        push(ready, axis, ring, way, r, pair)
+        ring.copy(way, r).start()
 
     def begin_chunk(ready, pair, d):
-        axis, ring = pair[2], pair[3][d]
-        return [push(ready, axis, ring, way, 0, pair) for way in ring.ways(0)]
-
-    starts = []
+        for way in pair[3][d].ways(0):
+            go(ready, pair[2], pair[3][d], way, 0, pair)
+
+    def arrived(pair, n, d):
+        key = (id(pair), d if d * 2 > -n else d + n)
+        missing[key] = missing.get(key, len(pair[3])) - 1
+        if missing[key] == 0 and pair[4] is not None:
+            pair[4](d)
+
     for pair in pairs:
-        starts += [push(0.0, pair[0], pair[1], way, 0, pair) for way in pair[1].ways(0)]
+        spread = isinstance(pair[1], Spread)
+        for r in range(pair[1].rounds if spread else 1):
+            for way in pair[1].ways(r):
+                if spread:
+                    push(0.0, pair[0], pair[1], way, r, pair, r + 1.0)
+                else:
+                    go(0.0, pair[0], pair[1], way, r, pair)
     for pair in pairs:
-        starts += begin_chunk(0.0, pair, 0)
-    for start in starts:
-        start()
+        begin_chunk(0.0, pair, 0)
+        arrived(pair, 2 * pair[3][0].rounds, 0)
     while events:
         event = min(events, key=lambda e: e[:2])
         events.remove(event)
-        order.append(event)
         now, _, ring, way, r, pair = event
         ring.copy(way, r, True).wait_recv()
-        starts = []
+        d = -(r + 1) if way == 0 else r + 1
         first = ring is pair[1]
-        if r + 1 < ring.rounds and way in ring.ways(r + 1):
-            starts.append(push(now, pair[0] if first else pair[2], ring, way, r + 1, pair))
+        if not (first and isinstance(ring, Spread)) and r + 1 < ring.rounds and way in ring.ways(r + 1):
+            go(now, pair[0] if first else pair[2], ring, way, r + 1, pair)
         if first:
-            starts += begin_chunk(now, pair, -(r + 1) if way == 0 else r + 1)
-        for start in starts:
-            start()
+            begin_chunk(now, pair, d)
+            arrived(pair, 2 * pair[3][0].rounds, 0)
+        else:
+            arrived(pair, 2 * ring.rounds, d)
 
 
 def gelu_value(pre_gelu):
@@ -211,15 +239,13 @@
     peer_recv,
     ring_send,
     ring_recv,
-    ex_send,
-    ex_recv,
     out_send,
     out_recv,
 ):
     at = Place(n_dp, y_hi)
     section = lax.axis_index("section")
     rows, width = x_in.shape
-    half = up_all.shape[4]
+    half = up_all.shape[2]
     features = normed_all.shape[3]
     hidden = act_all.shape[3]
     shard = up_ref.shape[0]
@@ -255,8 +281,9 @@
     def _():
         signal(barrier, after)
 
-    own_up = pltpu.make_async_copy(up_ref, up_all.at[at.lo, at.hi, at.z], load_sem.at[0])
-    own_down = pltpu.make_async_copy(down_ref, down_all.at[at.lo, at.hi, at.z], load_sem.at[1])
+    own_rows = pl.ds(pl.multiple_of(at.dp * shard, shard), shard)
+    own_up = pltpu.make_async_copy(up_ref, up_all.at[at.lo, own_rows], load_sem.at[0])
+    own_down = pltpu.make_async_copy(down_ref, down_all.at[at.lo, own_rows], load_sem.at[1])
     load_fst = pltpu.make_async_copy(fst_ref.at[:, mine], fst, load_sem.at[2])
     load_bst = pltpu.make_async_copy(bst_ref.at[:, mine], bst, load_sem.at[3])
     load_emb = pltpu.make_async_copy(emb_ref.at[mine], x_in, load_sem.at[4])
@@ -286,11 +313,14 @@
     bias_copy = remote(bias_all.at[at.lo], bias_all.at[at.lo], bias_sem.at[0], bias_sem.at[1], peer)
     bias_copy.start()
 
+    def shard_rows(y, z):
+        return pl.ds(pl.multiple_of(((y // Y_LO) * at.z_n + z) * shard, shard), shard)
+
     def up_slot(y, z):
-        return up_all.at[y % Y_LO, y // Y_LO, z]
+        return up_all.at[y % Y_LO, shard_rows(y, z)]
 
     def down_slot(y, z):
-        return down_all.at[y % Y_LO, y // Y_LO, z]
+        return down_all.at[y % Y_LO, shard_rows(y, z)]
 
     def fixed(slot, axis, step, d):
         there = step(d)
@@ -311,7 +341,7 @@
     if down_first.last_way == 1:
         down_then[at.z_n // 2] = down_then.pop(-(at.z_n // 2))
     weight_rings = [up_first, down_first, *up_then.values(), *down_then.values()]
-    run_gathers((("y", up_first, "z", up_then), ("z", down_first, "y", down_then)))
+    run_gathers((("y", up_first, "z", up_then, None), ("z", down_first, "y", down_then, None)))
 
     scale_f = jnp.transpose(fsc_ref[...].astype(F32))
     scale_b = jnp.transpose(bsc_ref[...].astype(F32))
@@ -332,16 +362,6 @@
     def columns(j):
         return pl.ds(pl.multiple_of(j * wide, wide), wide)
 
-    def up_weights(h):
-        return up_all[h].reshape(width, half)
-
-    def down_weights(h):
-        return down_all[h].reshape(width, half)
-
-    def quarter(ref, h, j):
-        count = y_hi // 2
-        return ref[h, pl.ds(j * count, count)].reshape(wide, half)
-
     def fwd_copy(j):
         return remote(code_f.at[:, columns(j)], x_in.at[:, columns(j)], hop_send.at[0, j], hop_recv.at[0, j], after)
 
@@ -358,71 +378,57 @@
         spot = (y % Y_LO) * at.y_hi_n + y // Y_LO
         return pl.ds(pl.multiple_of(spot * hidden, hidden), hidden)
 
-    def z_copy(k, src, dst, d):
-        target = at.step_z(d)
-        return remote(
-            src.at[:, feature_cols(target)], dst.at[at.y, at.z], ex_send.at[k, d], ex_recv.at[k, d], at.at_z(target)
-        )
-
-    def y_copy(k, src, dst, d):
-        target = at.step_y(d)
-        return remote(
-            src.at[:, hidden_cols(target)], dst.at[at.y, at.z], ex_send.at[k, d], ex_recv.at[k, d], at.at_y(target)
-        )
-
-    def z_start(k, src, dst):
-        for d in range(1, at.z_n):
-            z_copy(k, src, dst, d).start()
-        dst[at.y, at.z] = src[:, feature_cols(at.z)]
-
-    def y_start(k, src, dst):
-        for d in range(1, at.y_n):
-            y_copy(k, src, dst, d).start()
-        dst[at.y, at.z] = src[:, hidden_cols(at.y)]
-
-    def z_wait(k, dst):
-        for d in range(1, at.z_n):
-            spot = dst.at[at.y, at.step_z(-d)]
-            remote(spot, spot, ex_send.at[k, d], ex_recv.at[k, d], at.at_z(at.step_z(d))).wait_recv()
-
-    def y_wait(k, dst):
-        for d in range(1, at.y_n):
-            spot = dst.at[at.step_y(-d), at.z]
-            remote(spot, spot, ex_send.at[k, d], ex_recv.at[k, d], at.at_y(at.step_y(d))).wait_recv()
-
-    def ex_wait_send(k, copy, src, dst, n):
-        for d in range(1, n):
-            copy(k, src, dst, d).wait_send()
-
-    def row_rings(ref, first):
-        part = at.z_n // 2
-        return [
-            Ring(*y_ring, lambda y, c=c: ref.at[y, pl.ds(c * part, part)], at.at_y, sems, first + c, c) for c in range(2)
-        ]
-
-    def column_rings(ref, first):
-        part = at.y_n // 2
-        return [
-            Ring(*z_ring, lambda z, c=c: ref.at[pl.ds(c * part, part), z], at.at_z, sems, first + c, c) for c in range(2)
-        ]
-
-    normed_rings = row_rings(normed_all, index)
-    g_rings = row_rings(g_all, index + 2)
-    act_rings = column_rings(act_all, index + 4)
-    pg_rings = column_rings(pg_all, index + 6)
+    def exchange(src, dst, along_z, index, done=None):
+        if along_z:
+            spread = Spread(*z_ring, lambda z: src.at[:, feature_cols(z)], lambda z: dst.at[at.y, z], at.at_z, sems, index)
+            there, ring, device = at.step_z, y_ring, at.at_y
+        else:
+            spread = Spread(*y_ring, lambda y: src.at[:, hidden_cols(y)], lambda y: dst.at[y, at.z], at.at_y, sems, index)
+            there, ring, device = at.step_y, z_ring, at.at_z
+        n = z_ring[0] if along_z else y_ring[0]
+        rings = {}
+        for d in range(1 - n // 2, n // 2 + 1):
+            index += 1
+
+            def slot(i, d=d):
+                return dst.at[i, there(d)] if along_z else dst.at[there(d), i]
+
+            rings[d if d < n // 2 else -d] = Ring(*ring, slot, device, sems, index, index % 2)
+        axes = ("z", "y") if along_z else ("y", "z")
+        return (axes[0], spread, axes[1], rings, done)
+
+    def keep_own(src, dst, along_z):
+        dst[at.y, at.z] = src[:, feature_cols(at.z)] if along_z else src[:, hidden_cols(at.y)]
+
+    def add_column(d):
+        z = at.step_z(d)
+        left = normed_all[:, z].reshape(at.y_n * rows, features)
+        up_block[...] += inner(left, pg_all[:, z].reshape(at.y_n * rows, hidden))
+
+    def add_row(d):
+        y = at.step_y(d)
+        left = g_all[y].reshape(at.z_n * rows, features)
+        down_block[...] += inner(left, act_all[y].reshape(at.z_n * rows, hidden))
+
+    act_pair = exchange(act, act_all, False, index)
+    normed_pair = exchange(normed, normed_all, True, index + 1 + at.y_n)
+    pg_pair = exchange(pre_grad, pg_all, False, index + 2 + at.y_n + at.z_n, add_column)
+    g_pair = exchange(g_in, g_all, True, index + 3 + 2 * at.y_n + at.z_n, add_row)
+    early_pairs, late_pairs = (act_pair, normed_pair), (pg_pair, g_pair)
+
+    def wait_sends(pairs):
+        for pair in pairs:
+            for ring in (pair[1], *pair[3].values()):
+                ring.wait_send()
 
     def early():
-        y_start(2, act, act_all)
-        z_start(0, normed, normed_all)
+        start_spreads(early_pairs)
+        keep_own(act, act_all, False)
+        keep_own(normed, normed_all, True)
         for ring in weight_rings:
             ring.wait_send()
-        y_wait(2, act_all)
-        z_wait(0, normed_all)
-        run_rings(act_rings + normed_rings)
-        for ring in act_rings + normed_rings:
-            ring.wait_send()
-        ex_wait_send(0, z_copy, normed, normed_all, at.z_n)
-        ex_wait_send(2, y_copy, act, act_all, at.y_n)
+        run_gathers(early_pairs)
+        wait_sends(early_pairs)
 
     @pl.when(not_first)
     def _():
@@ -442,7 +448,7 @@
     inv[...] = jnp.broadcast_to(inverse, inv.shape)
 
     def up_half(h, _):
-        pre = jnp.dot(normed[...], up_weights(h), preferred_element_type=F32) + bias_all[h, 0:1, :]
+        pre = jnp.dot(normed[...], up_all[h], preferred_element_type=F32) + bias_all[h, 0:1, :]
         slope[:, hidden_half(h)] = pre
         act[:, hidden_half(h)] = gelu_value(pre).astype(BF16)
         return 0
@@ -451,7 +457,7 @@
 
     def down_half(j, _):
         cols = columns(j)
-        total = outer_t(act[:, :half], quarter(down_all, 0, j)) + outer_t(act[:, half:], quarter(down_all, 1, j))
+        total = outer_t(act[:, :half], down_all[0, cols, :]) + outer_t(act[:, half:], down_all[1, cols, :])
         output = (x_in[:, cols].astype(F32) + total + bdown_ref[:, cols]).astype(BF16)
         out_rows[:, cols] = output
         code_f[:, cols] = coded(output, fst[sid, :, cols], bound_f[:, cols])
@@ -488,17 +494,18 @@
         load_cot.wait()
 
     def up_grad_half(h, _):
-        act_grad = jnp.dot(g_in[...], down_weights(h), preferred_element_type=F32)
+        act_grad = jnp.dot(g_in[...], down_all[h], preferred_element_type=F32)
         pre_grad[:, hidden_half(h)] = (act_grad * slope[:, hidden_half(h)]).astype(BF16)
         return 0
 
     lax.fori_loop(0, 2, up_grad_half, 0)
-    y_start(3, pre_grad, pg_all)
-    z_start(1, g_in, g_all)
+    start_spreads(late_pairs)
+    keep_own(pre_grad, pg_all, False)
+    keep_own(g_in, g_all, True)
 
     def norm_grad_half(j, _):
         cols = columns(j)
-        total = outer_t(pre_grad[:, :half], quarter(up_all, 0, j)) + outer_t(pre_grad[:, half:], quarter(up_all, 1, j))
+        total = outer_t(pre_grad[:, :half], up_all[0, cols, :]) + outer_t(pre_grad[:, half:], up_all[1, cols, :])
         scaled[:, cols] = total * gain_ref[:, cols]
         return 0
 
@@ -530,27 +537,7 @@
 
     up_block[...] = jnp.zeros_like(up_block)
     down_block[...] = jnp.zeros_like(down_block)
-    y_wait(3, pg_all)
-    z_wait(1, g_all)
-
-    def add_column(z):
-        left = normed_all[:, z].reshape(at.y_n * rows, features)
-        up_block[...] += inner(left, pg_all[:, z].reshape(at.y_n * rows, hidden))
-
-    def add_row(y):
-        left = g_all[y].reshape(at.z_n * rows, features)
-        down_block[...] += inner(left, act_all[y].reshape(at.z_n * rows, hidden))
-
-    def add_round(r):
-        for n, step, add in ((at.z_n, at.step_z, add_column), (at.y_n, at.step_y, add_row)):
-            if r + 1 < n // 2:
-                lax.fori_loop(0, 2, lambda i, _, step=step, add=add: (add(step((2 * i - 1) * (r + 1))), 0)[1], 0)
-            elif r + 1 == n // 2:
-                add(step(r + 1))
-            if r == 0:
-                add(step(0))
-
-    run_rings(pg_rings + g_rings, add_round)
+    run_gathers(late_pairs)
 
     out_cols = pl.ds(pl.multiple_of(at.hi * hidden, hidden), hidden)
     outs = ((0, up_block, up_out), (1, down_block, down_out))
@@ -590,10 +577,7 @@
         for j in range(2):
             bwd_copy(j).wait_send()
 
-    ex_wait_send(1, z_copy, g_in, g_all, at.z_n)
-    ex_wait_send(3, y_copy, pre_grad, pg_all, at.y_n)
-    for ring in pg_rings + g_rings:
-        ring.wait_send()
+    wait_sends(late_pairs)
     remote(out_rows, out_ref.at[other], peer_send.at[0], peer_recv.at[0], peer).wait_recv()
     remote(ig_rows, ig_ref.at[other], peer_send.at[1], peer_recv.at[1], peer).wait_recv()
     out_copy.wait_send()
@@ -625,12 +609,8 @@
 
 def keep_kernel(*refs):
     count = len(refs) // 2
-    sems = refs[-1]
-    copies = [pltpu.make_async_copy(refs[i], refs[count + i], sems.at[i]) for i in range(count)]
-    for copy in copies:
-        copy.start()
-    for copy in copies:
-        copy.wait()
+    for source, target in zip(refs[:count], refs[count:]):
+        target[...] = source[...]
 
 
 def vmem(count):
@@ -670,9 +650,8 @@
     stored = fwd_store.shape[1]
     dma = pltpu.SemaphoreType.DMA
     rounds = max(y_n, z_n) // 2
-    n_rings = 2 + y_n + z_n + 8
-    peers = max(y_n, z_n)
-    whole = pltpu.VMEM((Y_LO, y_hi, z_n, shard, half), BF16)
+    n_rings = 6 + 3 * (y_n + z_n)
+    whole = pltpu.VMEM((Y_LO, width, half), BF16)
     narrow = pltpu.VMEM((rows, width), BF16)
     wide = pltpu.VMEM((rows, width), F32)
     outs = (
@@ -721,8 +700,6 @@
             dma((2,)),
             dma((n_rings, 2, rounds)),
             dma((n_rings, 2, rounds)),
-            dma((4, peers)),
-            dma((4, peers)),
             dma((2, y_hi)),
             dma((2, y_hi)),
         ],
@@ -747,9 +724,8 @@
     kept = pl.pallas_call(
         keep_kernel,
         out_shape=outs,
-        in_specs=anywhere(4),
-        out_specs=tuple(anywhere(4)),
-        scratch_shapes=[dma((4,))],
+        in_specs=vmem(4),
+        out_specs=tuple(vmem(4)),
     )(*results)
     return tuple(array[None] for array in kept)
 

time: 224 us -> 198 us (0.88)
  the two profiles are of different devices: /device:TPU:204 before, /device:TPU:12 now
where the time goes in v3:
time: 198 us
  Pallas kernels  197 us (99%)
    pallas_call x1, Pallas kernels, per_device(): pl.pallas_call(functools.partial(layer_kernel, n_sections, n_dp, y_hi), o...  195 us

profile of v3, /device:TPU:12, one launch (start us, length us, event | category | flops | bytes accessed | tf_op | source)
XLA Modules:
  0.0 198.0 jit_solution(14360449104707491942)
XLA Ops:
  1.3 194.7 %shard_map.156 = (bf16[128,1024]{1,0:T(8,128)(2,1)}, bf16[128,1024]{1,0:T(8,128)(2,1)}, f32[32,1024]{1,0:T(8,128)}, f32[32,1024]{1,0:T(8,128)}) custom-call(s32[1]{0:T(128)S(6)} %copy.17.sid_ref, bf16[128,1024]{1,0:T(8,128)(2,1)} %emb_ref.1, bf16[128,1024]{1,0:T(8,128)(2,1)} %cot_ref.1, bf16[32,1024]{1,0:T(8,128)(2,1)} %bitcast.18, ...), custom_call_target="tpu_custom_call" | custom-call | tf_op jit(solution)/shard_map/pallas_call | solution.py:663
  196.0 2.0 %shard_map.157 = (bf16[128,1024]{1,0:T(8,128)(2,1)}, bf16[128,1024]{1,0:T(8,128)(2,1)}, f32[32,1024]{1,0:T(8,128)}, f32[32,1024]{1,0:T(8,128)}) custom-call(bf16[128,1024]{1,0:T(8,128)(2,1)} %get-tuple-element.12.refs_0_, bf16[128,1024]{1,0:T(8,128)(2,1)} %get-tuple-element.13.refs_1_, f32[32,1024]{1,0:T(8,128)} %get-tuple-element.14.refs_2_, ...), custom_call_target="tpu_custom_call" | custom-call | tf_op jit(solution)/shard_map/pallas_call | solution.py:724

commit v4 on v3

--- a/solution.py
+++ b/solution.py
@@ -255,7 +255,8 @@
     other = pl.ds(pl.multiple_of((1 - at.lo) * rows, rows), rows)
     not_first = section > 0
     not_last = section < n_sections - 1
-    early_first = section < n_sections // 2
+    early_first = section <= n_sections // 2
+    early_after = jnp.logical_not(early_first)
     after = {"section": jnp.minimum(section + 1, n_sections - 1)}
     before = {"section": jnp.maximum(section - 1, 0)}
     peer = {"tensor": 1 - at.lo}
@@ -421,13 +422,14 @@
             for ring in (pair[1], *pair[3].values()):
                 ring.wait_send()
 
-    def early():
+    def early_spreads():
         start_spreads(early_pairs)
         keep_own(act, act_all, False)
         keep_own(normed, normed_all, True)
+
+    def early_sends():
         for ring in weight_rings:
             ring.wait_send()
-        run_gathers(early_pairs)
         wait_sends(early_pairs)
 
     @pl.when(not_first)
@@ -480,9 +482,14 @@
 
     lax.fori_loop(0, 2, slope_half, 0)
 
+    @pl.when(jnp.logical_or(early_first, not_last))
+    def _():
+        early_spreads()
+
     @pl.when(early_first)
     def _():
-        early()
+        run_gathers(early_pairs)
+        early_sends()
 
     @pl.when(not_last)
     def _():
@@ -531,13 +538,22 @@
     ig_copy = remote(ig_rows, ig_ref.at[mine], peer_send.at[1], peer_recv.at[1], peer)
     ig_copy.start()
 
-    @pl.when(jnp.logical_not(early_first))
-    def _():
-        early()
+    @pl.when(jnp.logical_and(early_after, jnp.logical_not(not_last)))
+    def _():
+        early_spreads()
 
     up_block[...] = jnp.zeros_like(up_block)
     down_block[...] = jnp.zeros_like(down_block)
-    run_gathers(late_pairs)
+    @pl.when(early_first)
+    def _():
+        run_gathers(late_pairs)
+
+    @pl.when(early_after)
+    def _():
+        run_gathers([pair[:4] + (None,) for pair in late_pairs + early_pairs])
+        lax.fori_loop(0, at.z_n, lambda d, _: (add_column(d), 0)[1], 0)
+        lax.fori_loop(0, at.y_n, lambda d, _: (add_row(d), 0)[1], 0)
+        early_sends()
 
     out_cols = pl.ds(pl.multiple_of(at.hi * hidden, hidden), hidden)
     outs = ((0, up_block, up_out), (1, down_block, down_out))

time: 198 us -> 192 us (0.970)
  the two profiles are of different devices: /device:TPU:12 before, /device:TPU:40 now
where the time goes in v4:
time: 192 us
  Pallas kernels  190 us (99%)
    pallas_call x1, Pallas kernels, per_device(): pl.pallas_call(functools.partial(layer_kernel, n_sections, n_dp, y_hi), o...  188 us

profile of v4, /device:TPU:40, one launch (start us, length us, event | category | flops | bytes accessed | tf_op | source)
XLA Modules:
  0.0 191.6 jit_solution(16267015596782244643)
XLA Ops:
  1.3 188.3 %shard_map.156 = (bf16[128,1024]{1,0:T(8,128)(2,1)}, bf16[128,1024]{1,0:T(8,128)(2,1)}, f32[32,1024]{1,0:T(8,128)}, f32[32,1024]{1,0:T(8,128)}) custom-call(s32[1]{0:T(128)S(6)} %copy.17.sid_ref, bf16[128,1024]{1,0:T(8,128)(2,1)} %emb_ref.1, bf16[128,1024]{1,0:T(8,128)(2,1)} %cot_ref.1, bf16[32,1024]{1,0:T(8,128)(2,1)} %bitcast.18, ...), custom_call_target="tpu_custom_call" | custom-call | tf_op jit(solution)/shard_map/pallas_call | solution.py:679
  189.6 2.0 %shard_map.157 = (bf16[128,1024]{1,0:T(8,128)(2,1)}, bf16[128,1024]{1,0:T(8,128)(2,1)}, f32[32,1024]{1,0:T(8,128)}, f32[32,1024]{1,0:T(8,128)}) custom-call(bf16[128,1024]{1,0:T(8,128)(2,1)} %get-tuple-element.12.refs_0_, bf16[128,1024]{1,0:T(8,128)(2,1)} %get-tuple-element.13.refs_1_, f32[32,1024]{1,0:T(8,128)} %get-tuple-element.14.refs_2_, ...), custom_call_target="tpu_custom_call" | custom-call | tf_op jit(solution)/shard_map/pallas_call | solution.py:740

commit v5 on v4

--- a/solution.py
+++ b/solution.py
@@ -12,6 +12,7 @@
 F32 = jnp.float32
 Y_LO = 2
 Y_HI = 4
+TURN = 24
 
 root_half = 0.7071067811865476
 density = 0.3989422804014327
@@ -110,7 +111,7 @@
                     pair[1].copy(way, r).start()
 
 
-def run_gathers(pairs, lag=1.0):
+def run_gathers(pairs, lag=1.0, midway=None):
     free, events, count, missing, brought = {}, [], [0], {}, {}
 
     def push(ready, axis, ring, way, r, pair, size=1.0):
@@ -144,12 +145,16 @@
     for pair in pairs:
         begin_chunk(0.0, pair, 0)
         arrived(pair, 2 * pair[3][0].rounds, 0)
+    arrivals = 0
     while events:
         event = min(events, key=lambda e: e[:2])
         events.remove(event)
         now, _, ring, way, r, pair = event
         ring.copy(way, r, True).wait_recv()
         d = -(r + 1) if way == 0 else r + 1
+        arrivals += 1
+        if midway is not None and arrivals == midway[0]:
+            midway[1]()
         first = ring is pair[1]
         if not (first and isinstance(ring, Spread)) and r + 1 < ring.rounds and way in ring.ways(r + 1):
             go(now, pair[0] if first else pair[2], ring, way, r + 1, pair)
@@ -207,6 +212,8 @@
     down_out,
     up_all,
     down_all,
+    up_turned,
+    down_turned,
     bias_all,
     x_in,
     g_in,
@@ -232,6 +239,7 @@
     up_block,
     down_block,
     load_sem,
+    turn_sem,
     bias_sem,
     hop_send,
     hop_recv,
@@ -342,7 +350,19 @@
     if down_first.last_way == 1:
         down_then[at.z_n // 2] = down_then.pop(-(at.z_n // 2))
     weight_rings = [up_first, down_first, *up_then.values(), *down_then.values()]
-    run_gathers((("y", up_first, "z", up_then, None), ("z", down_first, "y", down_then, None)))
+    weight_pairs = (("y", up_first, "z", up_then, None), ("z", down_first, "y", down_then, None))
+    even = section % 2 == 0
+
+    @pl.when(jnp.logical_not(even))
+    def _():
+        pl.semaphore_wait(turn_sem, 1)
+
+    def pass_turn():
+        @pl.when(jnp.logical_and(even, not_last))
+        def _():
+            pl.semaphore_signal(turn_sem, inc=1, device_id=after, device_id_type=MESH)
+
+    run_gathers(weight_pairs, midway=(TURN, pass_turn))
 
     scale_f = jnp.transpose(fsc_ref[...].astype(F32))
     scale_b = jnp.transpose(bsc_ref[...].astype(F32))
@@ -432,6 +452,24 @@
             ring.wait_send()
         wait_sends(early_pairs)
 
+    def turn(source, target):
+        count = half // 128
+
+        def body(i, _):
+            cols = pl.ds(pl.multiple_of((i % count) * 128, 128), 128)
+            target[i // count, cols, :] = jnp.transpose(source[i // count, :, cols])
+            return 0
+
+        lax.fori_loop(0, 2 * count, body, 0)
+
+    @pl.when(not_first)
+    def _():
+        turn(down_all, down_turned)
+
+    @pl.when(section > 1)
+    def _():
+        turn(up_all, up_turned)
+
     @pl.when(not_first)
     def _():
         for j in range(2):
@@ -449,17 +487,14 @@
     unit[...] = unit_values
     inv[...] = jnp.broadcast_to(inverse, inv.shape)
 
-    def up_half(h, _):
+    for h in range(2):
+        spot = pl.ds(h * half, half)
         pre = jnp.dot(normed[...], up_all[h], preferred_element_type=F32) + bias_all[h, 0:1, :]
-        slope[:, hidden_half(h)] = pre
-        act[:, hidden_half(h)] = gelu_value(pre).astype(BF16)
-        return 0
-
-    lax.fori_loop(0, 2, up_half, 0)
-
-    def down_half(j, _):
-        cols = columns(j)
-        total = outer_t(act[:, :half], down_all[0, cols, :]) + outer_t(act[:, half:], down_all[1, cols, :])
+        slope[:, spot] = pre
+        act[:, spot] = gelu_value(pre).astype(BF16)
+
+    def finish_output(j, total):
+        cols = pl.ds(j * wide, wide)
         output = (x_in[:, cols].astype(F32) + total + bdown_ref[:, cols]).astype(BF16)
         out_rows[:, cols] = output
         code_f[:, cols] = coded(output, fst[sid, :, cols], bound_f[:, cols])
@@ -468,14 +503,35 @@
         def _():
             fwd_copy(j).start()
 
-        return 0
-
-    lax.fori_loop(0, 2, down_half, 0)
+    def product_t(left, right, j):
+        cols = pl.ds(j * wide, wide)
+        return outer_t(left[:, :half], right[0, cols, :]) + outer_t(left[:, half:], right[1, cols, :])
+
+    def product(left, right, j):
+        cols = pl.ds(j * wide, wide)
+        return jnp.dot(left[:, :half], right[0, :, cols], preferred_element_type=F32) + jnp.dot(
+            left[:, half:], right[1, :, cols], preferred_element_type=F32
+        )
+
+    @pl.when(section == 0)
+    def _():
+        for j in range(2):
+            finish_output(j, product_t(act, down_all, j))
+
+    @pl.when(not_first)
+    def _():
+        for j in range(2):
+            finish_output(j, product(act, down_turned, j))
+
     out_keep = pltpu.make_async_copy(out_rows, out_ref.at[mine], load_sem.at[6])
     out_keep.start()
     out_copy = remote(out_rows, out_ref.at[mine], peer_send.at[0], peer_recv.at[0], peer)
     out_copy.start()
 
+    @pl.when(section <= 1)
+    def _():
+        turn(up_all, up_turned)
+
     def slope_half(h, _):
         slope[:, hidden_half(h)] = gelu_slope(slope[:, hidden_half(h)])
         return 0
@@ -500,23 +556,23 @@
     def _():
         load_cot.wait()
 
-    def up_grad_half(h, _):
+    for h in range(2):
+        spot = pl.ds(h * half, half)
         act_grad = jnp.dot(g_in[...], down_all[h], preferred_element_type=F32)
-        pre_grad[:, hidden_half(h)] = (act_grad * slope[:, hidden_half(h)]).astype(BF16)
-        return 0
-
-    lax.fori_loop(0, 2, up_grad_half, 0)
-    start_spreads(late_pairs)
-    keep_own(pre_grad, pg_all, False)
-    keep_own(g_in, g_all, True)
-
-    def norm_grad_half(j, _):
-        cols = columns(j)
-        total = outer_t(pre_grad[:, :half], up_all[0, cols, :]) + outer_t(pre_grad[:, half:], up_all[1, cols, :])
-        scaled[:, cols] = total * gain_ref[:, cols]
-        return 0
-
-    lax.fori_loop(0, 2, norm_grad_half, 0)
+        pre_grad[:, spot] = (act_grad * slope[:, spot]).astype(BF16)
+
+    def late_spreads():
+        start_spreads(late_pairs)
+        keep_own(pre_grad, pg_all, False)
+        keep_own(g_in, g_all, True)
+
+    @pl.when(section == 0)
+    def _():
+        late_spreads()
+
+    for j in range(2):
+        cols = pl.ds(j * wide, wide)
+        scaled[:, cols] = product(pre_grad, up_turned, j) * gain_ref[:, cols]
     scaled_values = scaled[...]
     unit_values = unit[...]
     first_mean = jnp.mean(scaled_values, axis=-1, keepdims=True)
@@ -532,6 +588,10 @@
         @pl.when(not_first)
         def _():
             bwd_copy(j).start()
+
+    @pl.when(not_first)
+    def _():
+        late_spreads()
 
     ig_keep = pltpu.make_async_copy(ig_rows, ig_ref.at[mine], load_sem.at[7])
     ig_keep.start()
@@ -684,6 +744,8 @@
         scratch_shapes=[
             whole,
             whole,
+            pltpu.VMEM((Y_LO, half, width), BF16),
+            pltpu.VMEM((Y_LO, half, width), BF16),
             pltpu.VMEM((Y_LO, 8, half), F32),
             narrow,
             narrow,
@@ -709,6 +771,7 @@
             pltpu.VMEM((features, hidden), F32),
             pltpu.VMEM((features, hidden), F32),
             dma((8,)),
+            pltpu.SemaphoreType.REGULAR,
             dma((2,)),
             dma((2, 2)),
             dma((2, 2)),

time: 192 us -> 187 us (0.974)
  the two profiles are of different devices: /device:TPU:40 before, /device:TPU:32 now
where the time goes in v5:
time: 187 us; the launch traced here: 186 us
  Pallas kernels  185 us (99%)
    pallas_call x1, Pallas kernels, per_device(): pl.pallas_call(functools.partial(layer_kernel, n_sections, n_dp, y_hi), o...  183 us

profile of v5, /device:TPU:32, one launch (start us, length us, event | category | flops | bytes accessed | tf_op | source)
XLA Modules:
  0.0 186.5 jit_solution(12985141451412236947)
XLA Ops:
  1.3 183.2 %shard_map.156 = (bf16[128,1024]{1,0:T(8,128)(2,1)}, bf16[128,1024]{1,0:T(8,128)(2,1)}, f32[32,1024]{1,0:T(8,128)}, f32[32,1024]{1,0:T(8,128)}) custom-call(s32[1]{0:T(128)S(6)} %copy.17.sid_ref, bf16[128,1024]{1,0:T(8,128)(2,1)} %emb_ref.1, bf16[128,1024]{1,0:T(8,128)(2,1)} %cot_ref.1, bf16[32,1024]{1,0:T(8,128)(2,1)} %bitcast.18, ...), custom_call_target="tpu_custom_call" | custom-call | tf_op jit(solution)/shard_map/pallas_call | solution.py:739
  184.5 2.0 %shard_map.157 = (bf16[128,1024]{1,0:T(8,128)(2,1)}, bf16[128,1024]{1,0:T(8,128)(2,1)}, f32[32,1024]{1,0:T(8,128)}, f32[32,1024]{1,0:T(8,128)}) custom-call(bf16[128,1024]{1,0:T(8,128)(2,1)} %get-tuple-element.12.refs_0_, bf16[128,1024]{1,0:T(8,128)(2,1)} %get-tuple-element.13.refs_1_, f32[32,1024]{1,0:T(8,128)} %get-tuple-element.14.refs_2_, ...), custom_call_target="tpu_custom_call" | custom-call | tf_op jit(solution)/shard_map/pallas_call | solution.py:803

commit v6 on v5

--- a/solution.py
+++ b/solution.py
@@ -263,7 +263,7 @@
     other = pl.ds(pl.multiple_of((1 - at.lo) * rows, rows), rows)
     not_first = section > 0
     not_last = section < n_sections - 1
-    early_first = section <= n_sections // 2
+    early_first = section < n_sections // 2
     early_after = jnp.logical_not(early_first)
     after = {"section": jnp.minimum(section + 1, n_sections - 1)}
     before = {"section": jnp.maximum(section - 1, 0)}

time: 187 us -> 185 us (0.989)
  the two profiles are of different devices: /device:TPU:32 before, /device:TPU:40 now
where the time goes in v6:
time: 185 us
  Pallas kernels  184 us (99%)
    pallas_call x1, Pallas kernels, per_device(): pl.pallas_call(functools.partial(layer_kernel, n_sections, n_dp, y_hi), o...  182 us

profile of v6, /device:TPU:40, one launch (start us, length us, event | category | flops | bytes accessed | tf_op | source)
XLA Modules:
  0.0 185.0 jit_solution(11170480570342696563)
XLA Ops:
  1.3 181.8 %shard_map.156 = (bf16[128,1024]{1,0:T(8,128)(2,1)}, bf16[128,1024]{1,0:T(8,128)(2,1)}, f32[32,1024]{1,0:T(8,128)}, f32[32,1024]{1,0:T(8,128)}) custom-call(s32[1]{0:T(128)S(6)} %copy.17.sid_ref, bf16[128,1024]{1,0:T(8,128)(2,1)} %emb_ref.1, bf16[128,1024]{1,0:T(8,128)(2,1)} %cot_ref.1, bf16[32,1024]{1,0:T(8,128)(2,1)} %bitcast.18, ...), custom_call_target="tpu_custom_call" | custom-call | tf_op jit(solution)/shard_map/pallas_call | solution.py:739
  183.1 2.0 %shard_map.157 = (bf16[128,1024]{1,0:T(8,128)(2,1)}, bf16[128,1024]{1,0:T(8,128)(2,1)}, f32[32,1024]{1,0:T(8,128)}, f32[32,1024]{1,0:T(8,128)}) custom-call(bf16[128,1024]{1,0:T(8,128)(2,1)} %get-tuple-element.12.refs_0_, bf16[128,1024]{1,0:T(8,128)(2,1)} %get-tuple-element.13.refs_1_, f32[32,1024]{1,0:T(8,128)} %get-tuple-element.14.refs_2_, ...), custom_call_target="tpu_custom_call" | custom-call | tf_op jit(solution)/shard_map/pallas_call | solution.py:803
